TPU v7x, 32 devices: a whole 2x2x4 slice. The times are simulated.
32 devices in a mesh: dp: 4 (over y, x), row: 4 (over z), col: 2 (over core).
Axes of the slice: x: 2, y: 2, z: 4, core: 2. Of those that a mesh axis runs over, the one named last changes fastest.
Arguments:
- tokens: bfloat16 [4096, 1088], P(('dp', 'row'), 'col'), may hold values from -64 to 64
- lengths: int32 [4, 2], P('dp'), may hold values from 0 to 1024, as said below
- first_gain: float32 [1088], P('col'), may hold values from 0.1 to 1.9
- first_shift: float32 [1088], P('col'), may hold values from -1.75 to 1.75
- qkv_weight: bfloat16 [1088, 3264], P('col', 'row'), may hold values from -0.1875 to 0.1875
- query_bias: float32 [1088], replicated, may hold values from -1.75 to 1.75
- value_bias: float32 [1088], replicated, may hold values from -1.75 to 1.75
- out_weight: bfloat16 [1088, 1088], P('row', 'col'), may hold values from -1 to 1
- out_bias: float32 [1088], P('col'), may hold values from -1.75 to 1.75
- second_gain: float32 [1088], P('col'), may hold values from 0.1 to 1.9
- second_shift: float32 [1088], P('col'), may hold values from -1.75 to 1.75
- up_weight: bfloat16 [1088, 4352], P('col', 'row'), may hold values from -0.1875 to 0.1875
- up_bias: float32 [4352], P('row'), may hold values from -1.75 to 1.75
- down_weight: bfloat16 [4352, 1088], P('row', 'col'), may hold values from -0.09375 to 0.09375
- down_bias: float32 [1088], P('col'), may hold values from -1.75 to 1.75
- cotangent: float32 [4096, 1088], P(('dp', 'row'), 'col'), may hold values from -6 to 6
Outputs:
- block_out: bfloat16 [4096, 1088], P(('dp', 'row'), 'col')
- input_grad: float32 [4096, 1088], P(('dp', 'row'), 'col')
- first_gain_grad: float32 [1088], P('col')
- first_shift_grad: float32 [1088], P('col')
- qkv_weight_grad: float32 [1088, 3264], P('col', 'row')
- query_bias_grad: float32 [1088], replicated
- value_bias_grad: float32 [1088], replicated
- out_weight_grad: float32 [1088, 1088], P('row', 'col')
- out_bias_grad: float32 [1088], P('col')
- second_gain_grad: float32 [1088], P('col')
- second_shift_grad: float32 [1088], P('col')
- up_weight_grad: float32 [1088, 4352], P('col', 'row')
- up_bias_grad: float32 [4352], P('row')
- down_weight_grad: float32 [4352, 1088], P('row', 'col')
- down_bias_grad: float32 [1088], P('col')
Inputs may be any that keep to these rules, and one draw needn't show every extreme that they name: Row g holds the lengths of the two sequences packed from the first slot of data group g; the first is longer than 896, the two together take at most 1024 slots, and the slots after them are padding.
All inputs are finite; a program needn't handle non-finite values.
Results may differ from a plain program's by a relative error of at most 0.012.
Values may be sent and summed in bfloat16 or wider, within the bound.
No kernel may reach another device: no remote copies, remote signals or barrier semaphores. Data moves between devices by JAX's collectives and lax.ppermute only.
A program may use at most 128 MiB of HBM per device.

v0:
```python
import jax
import jax.numpy as jnp
from jax import lax
from jax.sharding import PartitionSpec as P

D = 1088
HEADS = 17
HEAD_DIM = 64
FF = 4352
TOK_G = 1024


EPSILON = 1e-05
MASKED = -1e30


def width_sums(first_part, second_part):
    return lax.psum((first_part, second_part), "col")


def norm_forward(resid_in, norm_gain, norm_shift):
    total_sum, square_sum = width_sums(
        jnp.sum(resid_in, axis=1, keepdims=True),
        jnp.sum(resid_in * resid_in, axis=1, keepdims=True),
    )
    mean_value = total_sum / D
    inverse = lax.rsqrt(square_sum / D - mean_value * mean_value + EPSILON)
    normal = (resid_in - mean_value) * inverse
    return (normal * norm_gain + norm_shift, normal, inverse)


def norm_backward(grad_in, normal, inverse, norm_gain):
    scaled = grad_in * norm_gain
    mean_scaled, mean_cross = width_sums(
        jnp.sum(scaled, axis=1, keepdims=True), jnp.sum(scaled * normal, axis=1, keepdims=True)
    )
    grad_resid = inverse * (scaled - mean_scaled / D - normal * (mean_cross / D))
    return (grad_resid, jnp.sum(grad_in * normal, axis=0), jnp.sum(grad_in, axis=0))


def gather_rows(payload):
    return lax.all_gather(payload, "row", axis=0, tiled=True)


def gather_cols(payload):
    return lax.all_gather(payload, "col", axis=0, tiled=True)


def product(operand, weights, flipped):
    if flipped:
        return lax.dot_general(
            operand, weights, (((1,), (1,)), ((), ())), preferred_element_type=jnp.float32
        )
    return jnp.dot(operand, weights, preferred_element_type=jnp.float32)


def outer(operand, weights):
    return lax.dot_general(
        operand, weights, (((0,), (0,)), ((), ())), preferred_element_type=jnp.float32
    )


def scatter_cols(operand, weights, flipped):

    def partial_term(row_start, row_number):
        return product(operand, weights, flipped)

    return lax.psum_scatter(
        partial_term(
            jnp.int32(0), lax.axis_size("col") * (operand.shape[0] // lax.axis_size("col"))
        ),
        "col",
        scatter_dimension=0,
        tiled=True,
    )


def scatter_rows(operand, weights, flipped):

    def partial_term(row_start, row_number):
        return product(operand, weights, flipped)

    return lax.psum_scatter(
        partial_term(
            jnp.int32(0), lax.axis_size("row") * (operand.shape[0] // lax.axis_size("row"))
        ),
        "row",
        scatter_dimension=0,
        tiled=True,
    )


def to_heads(payload):
    return lax.all_to_all(payload, "row", split_axis=0, concat_axis=1, tiled=True)


def from_heads(payload):
    return lax.all_to_all(payload, "row", split_axis=1, concat_axis=0, tiled=True)


def gelu_tanh(pre_value):
    return jax.nn.gelu(pre_value, approximate=True)


def head_cols(matrix, offset, head_at):
    return lax.dynamic_slice_in_dim(matrix, offset + head_at * HEAD_DIM, HEAD_DIM, 1)


def place_part(vector, offset_block, length_all):
    return lax.dynamic_update_slice_in_dim(
        jnp.zeros((length_all,), jnp.float32), vector, offset_block * vector.shape[0], 0
    )


def on_device(
    tokens,
    lengths,
    first_gain,
    first_shift,
    qkv_weight,
    query_bias,
    value_bias,
    out_weight,
    out_bias,
    second_gain,
    second_shift,
    up_weight,
    up_bias,
    down_weight,
    down_bias,
    cotangent,
):
    row_devices = lax.axis_size("row")
    col_devices = lax.axis_size("col")
    row_index = lax.axis_index("row")
    col_index = lax.axis_index("col")
    local_rows = tokens.shape[0]
    block_rows = local_rows // col_devices
    half_width = tokens.shape[1]
    score_scale = HEAD_DIM ** (-0.5)
    first_len = lengths[0, 0]
    second_len = lengths[0, 1]

    def segment_of(positions):
        return (positions >= first_len).astype(jnp.int32) + (
            positions >= first_len + second_len
        ).astype(jnp.int32)

    block_index = col_index * row_devices + row_index
    query_pos = block_index * block_rows + jnp.arange(block_rows, dtype=jnp.int32)
    gathered = jnp.arange(TOK_G, dtype=jnp.int32)
    source = gathered // block_rows
    key_pos = (
        source % col_devices * row_devices + source // col_devices
    ) * block_rows + gathered % block_rows
    allowed = (key_pos[None, :] <= query_pos[:, None]) & (
        segment_of(key_pos)[None, :] == segment_of(query_pos)[:, None]
    )

    def masked_scores(query_head, key_head, allowed_pairs):
        raw_scores = (
            lax.dot_general(
                query_head, key_head, (((1,), (1,)), ((), ())), preferred_element_type=jnp.float32
            )
            * score_scale
        )
        return jnp.where(allowed_pairs, raw_scores, MASKED)

    def head_probs(query_head, key_head, allowed_pairs, top_score, row_total):
        return jnp.exp(masked_scores(query_head, key_head, allowed_pairs) - top_score) / row_total

    resid_in = tokens.astype(jnp.float32)
    normed_attn, normal_attn, inverse_attn = norm_forward(resid_in, first_gain, first_shift)
    attn_in = gather_rows(normed_attn.astype(jnp.bfloat16))
    qkv_part = scatter_cols(attn_in, qkv_weight, False)
    qkv_width = qkv_part.shape[1]
    bias_full = jnp.concatenate([query_bias, jnp.zeros_like(query_bias), value_bias])
    bias_here = lax.dynamic_slice_in_dim(bias_full, row_index * qkv_width, qkv_width)
    head_rows = to_heads((qkv_part + bias_here).astype(jnp.bfloat16))
    queries = head_rows[:, :D]
    key_value = head_rows[:, D:]
    all_keys = lax.all_gather(key_value, ("row", "col"), axis=0, tiled=True)

    def forward_head(head_at, carried):
        attention, row_tops, totals = carried
        scores = masked_scores(
            head_cols(queries, 0, head_at), head_cols(all_keys, 0, head_at), allowed
        )
        top_score = jnp.max(scores, axis=1, keepdims=True)
        exponent = jnp.exp(scores - top_score)
        row_total = jnp.sum(exponent, axis=1, keepdims=True)
        attn_probs = exponent / row_total
        result = jnp.dot(
            attn_probs.astype(jnp.bfloat16),
            head_cols(all_keys, D, head_at),
            preferred_element_type=jnp.float32,
        )
        attention = lax.dynamic_update_slice_in_dim(attention, result, head_at * HEAD_DIM, 1)
        row_tops = lax.dynamic_update_slice_in_dim(row_tops, top_score, head_at, 1)
        totals = lax.dynamic_update_slice_in_dim(totals, row_total, head_at, 1)
        return (attention, row_tops, totals)

    attention, row_tops, totals = lax.fori_loop(
        0,
        HEADS,
        forward_head,
        (
            jnp.zeros((block_rows, D), jnp.float32),
            jnp.zeros((block_rows, HEADS), jnp.float32),
            jnp.zeros((block_rows, HEADS), jnp.float32),
        ),
    )
    attn_full = gather_cols(from_heads(attention.astype(jnp.bfloat16)))
    resid_mid = resid_in + (scatter_rows(attn_full, out_weight, False) + out_bias)
    normed_mlp, normal_mlp, inverse_mlp = norm_forward(resid_mid, second_gain, second_shift)
    mlp_in = gather_rows(normed_mlp.astype(jnp.bfloat16))
    pre_act = scatter_cols(mlp_in, up_weight, False) + up_bias
    act_full = gather_cols(gelu_tanh(pre_act).astype(jnp.bfloat16))
    block_out = (resid_mid + (scatter_rows(act_full, down_weight, False) + down_bias)).astype(
        jnp.bfloat16
    )
    own_pos = row_index * local_rows + jnp.arange(local_rows, dtype=jnp.int32)
    live_rows = (segment_of(own_pos) < 2).astype(jnp.float32)
    grad_out = cotangent * live_rows[:, None]
    grad_out_low = grad_out.astype(jnp.bfloat16)
    down_bias_part = jnp.sum(grad_out_low, axis=0, dtype=jnp.float32)
    grad_out_full = gather_rows(grad_out_low)
    down_grad = outer(act_full, grad_out_full)
    grad_act = scatter_cols(grad_out_full, down_weight, True)
    gelu_value, gelu_back = jax.vjp(gelu_tanh, pre_act)
    grad_pre = gelu_back(grad_act)[0].astype(jnp.bfloat16)
    up_bias_part = jnp.sum(grad_pre, axis=0, dtype=jnp.float32)
    grad_pre_full = gather_cols(grad_pre)
    up_grad = outer(mlp_in, grad_pre_full)
    grad_normed_mlp = scatter_rows(grad_pre_full, up_weight, True)
    back_mlp, second_gain_part, second_shift_part = norm_backward(
        grad_normed_mlp, normal_mlp, inverse_mlp, second_gain
    )
    grad_mid = grad_out + back_mlp
    grad_mid_low = grad_mid.astype(jnp.bfloat16)
    out_bias_part = jnp.sum(grad_mid_low, axis=0, dtype=jnp.float32)
    grad_mid_full = gather_rows(grad_mid_low)
    out_grad = outer(attn_full, grad_mid_full)
    grad_heads = to_heads(scatter_cols(grad_mid_full, out_weight, True).astype(jnp.bfloat16))

    def backward_head(head_at, carried):
        grad_query, grad_key_value, deltas = carried
        query_head = head_cols(queries, 0, head_at)
        key_head = head_cols(all_keys, 0, head_at)
        grad_head = head_cols(grad_heads, 0, head_at)
        attn_probs = head_probs(
            query_head,
            key_head,
            allowed,
            lax.dynamic_slice_in_dim(row_tops, head_at, 1, 1),
            lax.dynamic_slice_in_dim(totals, head_at, 1, 1),
        )
        grad_probs = product(grad_head, head_cols(all_keys, D, head_at), True)
        row_delta = jnp.sum(attn_probs * grad_probs, axis=1, keepdims=True)
        grad_scores = (attn_probs * (grad_probs - row_delta)).astype(jnp.bfloat16)
        query_part = (
            jnp.dot(grad_scores, key_head, preferred_element_type=jnp.float32) * score_scale
        )
        grad_query = lax.dynamic_update_slice_in_dim(grad_query, query_part, head_at * HEAD_DIM, 1)
        deltas = lax.dynamic_update_slice_in_dim(deltas, row_delta, head_at, 1)
        value_part = outer(attn_probs.astype(jnp.bfloat16), grad_head)
        key_part = outer(grad_scores, query_head) * score_scale
        summed = lax.psum_scatter(
            jnp.concatenate([key_part, value_part], axis=1),
            ("row", "col"),
            scatter_dimension=0,
            tiled=True,
        )
        grad_key_value = lax.dynamic_update_slice_in_dim(
            grad_key_value, summed[:, :HEAD_DIM], head_at * HEAD_DIM, 1
        )
        grad_key_value = lax.dynamic_update_slice_in_dim(
            grad_key_value, summed[:, HEAD_DIM:], D + head_at * HEAD_DIM, 1
        )
        return (grad_query, grad_key_value, deltas)

    grad_query, grad_key_value, deltas = lax.fori_loop(
        0,
        HEADS,
        backward_head,
        (
            jnp.zeros((block_rows, D), jnp.float32),
            jnp.zeros((block_rows, 2 * D), jnp.float32),
            jnp.zeros((block_rows, HEADS), jnp.float32),
        ),
    )
    grad_queries = grad_query.astype(jnp.bfloat16)
    grad_kv_low = grad_key_value.astype(jnp.bfloat16)
    query_bias_part = jnp.sum(grad_queries, axis=0, dtype=jnp.float32)
    value_bias_part = jnp.sum(grad_kv_low[:, D:], axis=0, dtype=jnp.float32)
    grad_qkv_full = gather_cols(from_heads(jnp.concatenate([grad_queries, grad_kv_low], axis=1)))
    qkv_grad = outer(attn_in, grad_qkv_full)
    grad_normed_attn = scatter_rows(grad_qkv_full, qkv_weight, True)
    back_attn, first_gain_part, first_shift_part = norm_backward(
        grad_normed_attn, normal_attn, inverse_attn, first_gain
    )
    input_grad = grad_mid + back_attn
    qkv_grad, out_grad, up_grad, down_grad = lax.psum(
        (qkv_grad, out_grad, up_grad, down_grad), "dp"
    )
    summed_small = lax.psum(
        (
            place_part(first_gain_part, col_index, D),
            place_part(first_shift_part, col_index, D),
            query_bias_part,
            value_bias_part,
            place_part(out_bias_part, col_index, D),
            place_part(second_gain_part, col_index, D),
            place_part(second_shift_part, col_index, D),
            place_part(up_bias_part, row_index, FF),
            place_part(down_bias_part, col_index, D),
        ),
        ("dp", "row", "col"),
    )

    def own_half(vector):
        return lax.dynamic_slice_in_dim(vector, col_index * half_width, half_width)

    up_width = up_bias.shape[0]
    return (
        block_out,
        input_grad,
        own_half(summed_small[0]),
        own_half(summed_small[1]),
        qkv_grad,
        summed_small[2],
        summed_small[3],
        out_grad,
        own_half(summed_small[4]),
        own_half(summed_small[5]),
        own_half(summed_small[6]),
        up_grad,
        lax.dynamic_slice_in_dim(summed_small[7], row_index * up_width, up_width),
        down_grad,
        own_half(summed_small[8]),
    )


def solution(mesh):
    in_specs = (
        P(("dp", "row"), "col"),
        P("dp", None),
        P("col"),
        P("col"),
        P("col", "row"),
        P(),
        P(),
        P("row", "col"),
        P("col"),
        P("col"),
        P("col"),
        P("col", "row"),
        P("row"),
        P("row", "col"),
        P("col"),
        P(("dp", "row"), "col"),
    )
    out_specs = (
        P(("dp", "row"), "col"),
        P(("dp", "row"), "col"),
        P("col"),
        P("col"),
        P("col", "row"),
        P(),
        P(),
        P("row", "col"),
        P("col"),
        P("col"),
        P("col"),
        P("col", "row"),
        P("row"),
        P("row", "col"),
        P("col"),
    )
    return jax.shard_map(
        on_device, mesh=mesh, in_specs=in_specs, out_specs=out_specs, check_vma=False
    )
```

profile of v0, /device:TPU:0, one launch (start us, length us, event | category | flops | bytes accessed | tf_op | source)
XLA Modules:
  0.0 1473.8 jit_solution(11749053921107545506)
XLA Ops:
  13.0 33.8 %all-gather.9.cloned.1.call-done = bf16[1024,544]{0,1:T(8,128)(2,1)} async-done(((bf16[256,544]{0,1:T(8,128)(2,1)}), bf16[1024,544]{0,1:T(8,128)(2,1)}) %all-gather.9.cloned.1.call-update) | async-done | bytes 1114128 | tf_op jit(solution)/shard_map/all_gather | solution.py:42
  46.7 4.7 fusion.80
  52.4 8.8 reduce-scatter.10.cloned.1.call-done
  62.8 26.3 %all_to_all.76 = bf16[4,128,816]{1,2,0:T(8,128)(2,1)S(1)} all-to-all(bf16[4,128,816]{1,2,0:T(8,128)(2,1)S(1)} %copy_bitcast_fusion.1), channel_id=1, replica_groups=mesh['dp'=4,'row'=4,'col'=2] {'row'}, dimensions={0} | all-to-all | bytes 1671168 | tf_op jit(solution)/shard_map/all_to_all | solution.py:94
  93.5 45.6 %all-gather.11.cloned.1.call-done = bf16[1024,2176]{0,1:T(8,128)(2,1)} async-done(((bf16[128,2176]{0,1:T(8,128)(2,1)}), bf16[1024,2176]{0,1:T(8,128)(2,1)}) %all-gather.11.cloned.1.call-update) | async-done | bytes 4456464 | tf_op jit(solution)/shard_map/all_gather | solution.py:182
  139.1 6.6 copy.44
  145.7 94.1 %while.38 = (s32[]{:T(128)}, bf16[128,1088]{0,1:T(8,128)(2,1)S(1)}, f32[128,17]{0,1:T(8,128)}, f32[128,17]{0,1:T(8,128)}, bf16[128,1088]{1,0:T(8,128)(2,1)S(1)},...) while((s32[]{:T(128)}, bf16[128,1088]{0,1:T(8,128)(2,1)S(1)}, ...), condition=%wide.region_8.9_spmd.clone, body=%wide.region_5.8_spmd.clone.sunk | while | flops 34995976 | bytes 2176798 | solution.py:203
  239.8 12.3 all_to_all.77
  259.3 42.5 %reduce-scatter.12.cloned.1.call-done = f32[256,544]{0,1:T(8,128)} async-done(((f32[1024,544]{0,1:T(8,128)}), f32[256,544]{0,1:T(8,128)}) %reduce-scatter.12.cloned.1.call-update) | async-done | bytes 557072 | tf_op jit(solution)/shard_map/reduce_scatter | solution.py:83
  309.7 24.7 %all-gather.17.cloned.1.call-done = bf16[1024,544]{0,1:T(8,128)(2,1)} async-done(((bf16[256,544]{0,1:T(8,128)(2,1)}), bf16[1024,544]{0,1:T(8,128)(2,1)}) %all-gather.17.cloned.1.call-update) | async-done | bytes 1114128 | tf_op jit(solution)/shard_map/all_gather | solution.py:42
  334.4 5.7 fusion.83
  340.1 25.7 %all-gather.13.cloned.1.call-done = bf16[1024,544]{0,1:T(8,128)(2,1)} async-done(((bf16[256,544]{0,1:T(8,128)(2,1)}), bf16[1024,544]{0,1:T(8,128)(2,1)}) %all-gather.13.cloned.1.call-update) | async-done | bytes 1114128 | tf_op jit(solution)/shard_map/all_gather | solution.py:42
  365.9 5.3 fusion.82
  371.3 7.6 reduce-scatter.18.cloned.1.call-done
  378.9 15.9 %reduce-scatter.14.cloned.1.call-done = f32[512,1088]{0,1:T(8,128)} async-done(((f32[1024,1088]{0,1:T(8,128)}), f32[512,1088]{0,1:T(8,128)}) %reduce-scatter.14.cloned.1.call-update) | async-done | bytes 2228240 | tf_op jit(solution)/shard_map/reduce_scatter | solution.py:68
  394.8 6.1 convert_reduce_fusion
  401.7 11.3 all-gather.19.cloned.1.call-done
  417.7 9.3 all-gather.15.cloned.1.call-done
  431.7 45.5 %reduce-scatter.20.cloned.1.call-done = f32[256,544]{0,1:T(8,128)} async-done(((f32[1024,544]{0,1:T(8,128)}), f32[256,544]{0,1:T(8,128)}) %reduce-scatter.20.cloned.1.call-update) | async-done | bytes 557072 | tf_op jit(solution)/shard_map/reduce_scatter | solution.py:83
  481.1 44.4 %reduce-scatter.16.cloned.1.call-done = f32[256,544]{0,1:T(8,128)} async-done(((f32[1024,544]{0,1:T(8,128)}), f32[256,544]{0,1:T(8,128)}) %reduce-scatter.16.cloned.1.call-update) | async-done | bytes 557072 | tf_op jit(solution)/shard_map/reduce_scatter | solution.py:83
  528.2 30.6 %all-gather.21.cloned.1.call-done = bf16[1024,544]{0,1:T(8,128)(2,1)} async-done(((bf16[256,544]{0,1:T(8,128)(2,1)}), bf16[1024,544]{0,1:T(8,128)(2,1)}) %all-gather.21.cloned.1.call-update) | async-done | bytes 1114128 | tf_op jit(solution)/shard_map/all_gather | solution.py:42
  561.6 7.1 reduce-scatter.22.cloned.1.call-done
  570.5 4.9 all-to-all-start.2
  575.4 9.7 all-to-all-done.2
  585.2 621.3 %while.39 = (s32[]{:T(128)}, bf16[128,1088]{0,1:T(8,128)(2,1)S(1)}, bf16[128,2176]{0,1:T(8,128)(2,1)S(1)}, bf16[128,1088]{1,0:T(8,128)(2,1)}, bf16[1024,2176]{1,...) while((s32[]{:T(128)}, bf16[128,1088]{0,1:T(8,128)(2,1)S(1)}, ...), condition=%wide.region_26.27_spmd.clone, body=%wide.region_23.26_spmd.clone.sunk | while | flops 85794696 | bytes 8271202 | solution.py:282
  592.3 28.8 %reduce-scatter.26.cloned.1.call-done = f32[128,128]{0,1:T(8,128)} async-done(((f32[1024,128]{0,1:T(8,128)}), f32[128,128]{0,1:T(8,128)}) %reduce-scatter.26.cloned.1.call-update) | async-done | bytes 65552 | tf_op jit(solution)/shard_map/while/body/eval_jaxpr/reduce_scatter | solution.py:268
  629.7 28.0 %reduce-scatter.26.cloned.1.call-done = f32[128,128]{0,1:T(8,128)} async-done(((f32[1024,128]{0,1:T(8,128)}), f32[128,128]{0,1:T(8,128)}) %reduce-scatter.26.cloned.1.call-update) | async-done | bytes 65552 | tf_op jit(solution)/shard_map/while/body/eval_jaxpr/reduce_scatter | solution.py:268
  666.2 27.9 %reduce-scatter.26.cloned.1.call-done = f32[128,128]{0,1:T(8,128)} async-done(((f32[1024,128]{0,1:T(8,128)}), f32[128,128]{0,1:T(8,128)}) %reduce-scatter.26.cloned.1.call-update) | async-done | bytes 65552 | tf_op jit(solution)/shard_map/while/body/eval_jaxpr/reduce_scatter | solution.py:268
  702.7 27.9 %reduce-scatter.26.cloned.1.call-done = f32[128,128]{0,1:T(8,128)} async-done(((f32[1024,128]{0,1:T(8,128)}), f32[128,128]{0,1:T(8,128)}) %reduce-scatter.26.cloned.1.call-update) | async-done | bytes 65552 | tf_op jit(solution)/shard_map/while/body/eval_jaxpr/reduce_scatter | solution.py:268
  739.2 27.9 %reduce-scatter.26.cloned.1.call-done = f32[128,128]{0,1:T(8,128)} async-done(((f32[1024,128]{0,1:T(8,128)}), f32[128,128]{0,1:T(8,128)}) %reduce-scatter.26.cloned.1.call-update) | async-done | bytes 65552 | tf_op jit(solution)/shard_map/while/body/eval_jaxpr/reduce_scatter | solution.py:268
  775.7 27.9 %reduce-scatter.26.cloned.1.call-done = f32[128,128]{0,1:T(8,128)} async-done(((f32[1024,128]{0,1:T(8,128)}), f32[128,128]{0,1:T(8,128)}) %reduce-scatter.26.cloned.1.call-update) | async-done | bytes 65552 | tf_op jit(solution)/shard_map/while/body/eval_jaxpr/reduce_scatter | solution.py:268
  812.1 27.9 %reduce-scatter.26.cloned.1.call-done = f32[128,128]{0,1:T(8,128)} async-done(((f32[1024,128]{0,1:T(8,128)}), f32[128,128]{0,1:T(8,128)}) %reduce-scatter.26.cloned.1.call-update) | async-done | bytes 65552 | tf_op jit(solution)/shard_map/while/body/eval_jaxpr/reduce_scatter | solution.py:268
  848.6 27.9 %reduce-scatter.26.cloned.1.call-done = f32[128,128]{0,1:T(8,128)} async-done(((f32[1024,128]{0,1:T(8,128)}), f32[128,128]{0,1:T(8,128)}) %reduce-scatter.26.cloned.1.call-update) | async-done | bytes 65552 | tf_op jit(solution)/shard_map/while/body/eval_jaxpr/reduce_scatter | solution.py:268
  885.0 27.9 %reduce-scatter.26.cloned.1.call-done = f32[128,128]{0,1:T(8,128)} async-done(((f32[1024,128]{0,1:T(8,128)}), f32[128,128]{0,1:T(8,128)}) %reduce-scatter.26.cloned.1.call-update) | async-done | bytes 65552 | tf_op jit(solution)/shard_map/while/body/eval_jaxpr/reduce_scatter | solution.py:268
  921.5 27.9 %reduce-scatter.26.cloned.1.call-done = f32[128,128]{0,1:T(8,128)} async-done(((f32[1024,128]{0,1:T(8,128)}), f32[128,128]{0,1:T(8,128)}) %reduce-scatter.26.cloned.1.call-update) | async-done | bytes 65552 | tf_op jit(solution)/shard_map/while/body/eval_jaxpr/reduce_scatter | solution.py:268
  958.0 27.9 %reduce-scatter.26.cloned.1.call-done = f32[128,128]{0,1:T(8,128)} async-done(((f32[1024,128]{0,1:T(8,128)}), f32[128,128]{0,1:T(8,128)}) %reduce-scatter.26.cloned.1.call-update) | async-done | bytes 65552 | tf_op jit(solution)/shard_map/while/body/eval_jaxpr/reduce_scatter | solution.py:268
  994.5 28.0 %reduce-scatter.26.cloned.1.call-done = f32[128,128]{0,1:T(8,128)} async-done(((f32[1024,128]{0,1:T(8,128)}), f32[128,128]{0,1:T(8,128)}) %reduce-scatter.26.cloned.1.call-update) | async-done | bytes 65552 | tf_op jit(solution)/shard_map/while/body/eval_jaxpr/reduce_scatter | solution.py:268
  1031.0 27.9 %reduce-scatter.26.cloned.1.call-done = f32[128,128]{0,1:T(8,128)} async-done(((f32[1024,128]{0,1:T(8,128)}), f32[128,128]{0,1:T(8,128)}) %reduce-scatter.26.cloned.1.call-update) | async-done | bytes 65552 | tf_op jit(solution)/shard_map/while/body/eval_jaxpr/reduce_scatter | solution.py:268
  1067.5 27.9 %reduce-scatter.26.cloned.1.call-done = f32[128,128]{0,1:T(8,128)} async-done(((f32[1024,128]{0,1:T(8,128)}), f32[128,128]{0,1:T(8,128)}) %reduce-scatter.26.cloned.1.call-update) | async-done | bytes 65552 | tf_op jit(solution)/shard_map/while/body/eval_jaxpr/reduce_scatter | solution.py:268
  1104.0 28.0 %reduce-scatter.26.cloned.1.call-done = f32[128,128]{0,1:T(8,128)} async-done(((f32[1024,128]{0,1:T(8,128)}), f32[128,128]{0,1:T(8,128)}) %reduce-scatter.26.cloned.1.call-update) | async-done | bytes 65552 | tf_op jit(solution)/shard_map/while/body/eval_jaxpr/reduce_scatter | solution.py:268
  1140.5 27.9 %reduce-scatter.26.cloned.1.call-done = f32[128,128]{0,1:T(8,128)} async-done(((f32[1024,128]{0,1:T(8,128)}), f32[128,128]{0,1:T(8,128)}) %reduce-scatter.26.cloned.1.call-update) | async-done | bytes 65552 | tf_op jit(solution)/shard_map/while/body/eval_jaxpr/reduce_scatter | solution.py:268
  1177.0 28.0 %reduce-scatter.26.cloned.1.call-done = f32[128,128]{0,1:T(8,128)} async-done(((f32[1024,128]{0,1:T(8,128)}), f32[128,128]{0,1:T(8,128)}) %reduce-scatter.26.cloned.1.call-update) | async-done | bytes 65552 | tf_op jit(solution)/shard_map/while/body/eval_jaxpr/reduce_scatter | solution.py:268
  1206.5 23.1 %all_to_all.78 = bf16[128,4,816]{0,2,1:T(8,128)(2,1)S(1)} all-to-all(bf16[128,4,816]{0,2,1:T(8,128)(2,1)S(1)} %bitcast.92), channel_id=1, replica_groups=mesh['dp'=4,'row'=4,'col'=2] {'row'}, dimensions={1} | all-to-all | bytes 1671168 | tf_op jit(solution)/shard_map/all_to_all | solution.py:98
  1230.7 9.2 all-gather.23.cloned.1.call-done
  1244.4 5.2 fusion.86
  1259.3 32.2 %reduce-scatter.24.cloned.1.call-done = f32[256,544]{0,1:T(8,128)} async-done(((f32[1024,544]{0,1:T(8,128)}), f32[256,544]{0,1:T(8,128)}) %reduce-scatter.24.cloned.1.call-update) | async-done | bytes 557072 | tf_op jit(solution)/shard_map/reduce_scatter | solution.py:83
  1293.5 42.4 %all-reduce = (f32[1088]{0:T(1024)S(1)}, f32[1088]{0:T(1024)S(1)}, f32[1088]{0:T(1024)}, f32[1088]{0:T(1024)}, f32[1088]{0:T(1024)S(1)}, /*index=5*/f32[1088]{0:...) all-reduce(f32[1088]{0:T(1024)S(1)} %dynamic_update_slice.81, ...), channel_id=1, replica_groups=mesh['dp'=4,'row'=4,'col'=2] {'dp','row','col'}, use_global_device_ids=true, to_apply=%region_33.34 | all-reduce | flops 13056 | bytes 104448 | tf_op jit(solution)/shard_map/psum | solution.py:306
  1345.1 113.8 %all-reduce.8.cloned.1.call-done = (f32[544,816]{1,0:T(8,128)}, f32[272,544]{1,0:T(8,128)}, f32[544,1088]{1,0:T(8,128)}, f32[1088,544]{0,1:T(8,128)}) async-done(((f32[544,816]{1,0:T(8,128)}, f32[272,544]{1,0:T(8,128)}, f32[544,1088]{1,0:T(8,128)}, f32[1088,544]{0,1:T(8,128)}), (f32[544,816]{1,0:T(8,128)}, f32[272,544]{1,0:T(8,128)}, f32[544,1088]{1,0:T(8,128)}, ...) | async-done | bytes 7102480 | tf_op jit(solution)/shard_map/psum | solution.py:303
  (485 shorter events, 320.8 us)
Async XLA Ops:
  7.2 358.7 %copy-start = (bf16[544,1088]{1,0:T(8,128)(2,1)S(1)}, bf16[544,1088]{1,0:T(8,128)(2,1)}, u32[]{:S(2)}) copy-start(bf16[544,1088]{1,0:T(8,128)(2,1)} %param.31) | copy-start | bytes 3551236
  7.2 39.5 %all-gather.9.cloned.1.call-start = ((), (), s32[]{:S(2)}) async-start(), calls=%async_computation.13 | async-start | bytes 1392640 | tf_op jit(solution)/shard_map/all_gather | solution.py:42
  11.0 40.5 %copy-start.14 = (f32[256,1]{0,1:T(1,128)}, f32[256,1]{0,1:T(1,128)S(1)}, u32[]{:S(2)}) copy-start(f32[256,1]{0,1:T(1,128)S(1)} %get-tuple-element.614) | copy-start | bytes 3076
  11.0 40.5 %copy-start.16 = (f32[256,1]{0,1:T(1,128)}, f32[256,1]{0,1:T(1,128)S(1)}, u32[]{:S(2)}) copy-start(f32[256,1]{0,1:T(1,128)S(1)} %get-tuple-element.615) | copy-start | bytes 3076
  12.9 48.2 %reduce-scatter.10.cloned.1.call-start = ((), (), s32[]{:S(2)}) async-start(), calls=%async_computation.14 | async-start | bytes 5013504 | tf_op jit(solution)/shard_map/reduce_scatter | solution.py:68
  51.5 87.6 %all-gather.11.cloned.1.call-start = ((), (), s32[]{:S(2)}) async-start(), calls=%async_computation.15 | async-start | bytes 5013504 | tf_op jit(solution)/shard_map/all_gather | solution.py:182
  90.0 211.8 %reduce-scatter.12.cloned.1.call-start = ((), (), s32[]{:S(2)}) async-start(), calls=%async_computation.16 | async-start | bytes 2785280 | tf_op jit(solution)/shard_map/reduce_scatter | solution.py:83
  145.7 108.7 %copy-start.8 = (bf16[272,544]{1,0:T(8,128)(2,1)S(1)}, bf16[272,544]{1,0:T(8,128)(2,1)}, u32[]{:S(2)}) copy-start(bf16[272,544]{1,0:T(8,128)(2,1)} %param.27) | copy-start | bytes 887812
  256.5 45.2 %copy-start.2 = (bf16[256,544]{0,1:T(8,128)(2,1)S(1)}, bf16[256,544]{0,1:T(8,128)(2,1)}, u32[]{:S(2)}) copy-start(bf16[256,544]{0,1:T(8,128)(2,1)} %param.20) | copy-start | bytes 835588
  256.5 51.5 %copy-start.11 = (f32[544]{0:T(1024)S(1)}, f32[544]{0:T(1024)}, u32[]{:S(2)}) copy-start(f32[544]{0:T(1024)} %param.29) | copy-start | bytes 6532
  256.6 77.8 %all-gather.17.cloned.1.call-start = ((), (), s32[]{:S(2)}) async-start(), calls=%async_computation.21 | async-start | bytes 1392640 | tf_op jit(solution)/shard_map/all_gather | solution.py:42
  259.2 106.6 %all-gather.13.cloned.1.call-start = ((), (), s32[]{:S(2)}) async-start(), calls=%async_computation.17 | async-start | bytes 1392640 | tf_op jit(solution)/shard_map/all_gather | solution.py:42
  309.6 69.2 %reduce-scatter.18.cloned.1.call-start = ((), (), s32[]{:S(2)}) async-start(), calls=%async_computation.22 | async-start | bytes 6684672 | tf_op jit(solution)/shard_map/reduce_scatter | solution.py:68
  340.1 54.8 %reduce-scatter.14.cloned.1.call-start = ((), (), s32[]{:S(2)}) async-start(), calls=%async_computation.18 | async-start | bytes 6684672 | tf_op jit(solution)/shard_map/reduce_scatter | solution.py:68
  371.2 41.8 %all-gather.19.cloned.1.call-start = ((), (), s32[]{:S(2)}) async-start(), calls=%async_computation.23 | async-start | bytes 3342336 | tf_op jit(solution)/shard_map/all_gather | solution.py:46
  400.9 26.1 %all-gather.15.cloned.1.call-start = ((), (), s32[]{:S(2)}) async-start(), calls=%async_computation.19 | async-start | bytes 3342336 | tf_op jit(solution)/shard_map/all_gather | solution.py:46
  401.5 75.7 %reduce-scatter.20.cloned.1.call-start = ((), (), s32[]{:S(2)}) async-start(), calls=%async_computation.24 | async-start | bytes 2785280 | tf_op jit(solution)/shard_map/reduce_scatter | solution.py:83
  417.7 107.9 %reduce-scatter.16.cloned.1.call-start = ((), (), s32[]{:S(2)}) async-start(), calls=%async_computation.20 | async-start | bytes 2785280 | tf_op jit(solution)/shard_map/reduce_scatter | solution.py:83
  431.6 45.6 %copy-start.20 = (f32[256,1]{0,1:T(1,128)S(1)}, f32[256,1]{0,1:T(1,128)}, u32[]{:S(2)}) copy-start(f32[256,1]{0,1:T(1,128)} %copy-done.19) | copy-start | bytes 3076
  431.6 45.6 %copy-start.22 = (f32[256,1]{0,1:T(1,128)S(1)}, f32[256,1]{0,1:T(1,128)}, u32[]{:S(2)}) copy-start(f32[256,1]{0,1:T(1,128)} %copy-done.21) | copy-start | bytes 3076
  431.6 93.9 %copy-start.24 = (f32[256]{0:T(256)S(1)}, f32[256]{0:T(256)}, u32[]{:S(2)}) copy-start(f32[256]{0:T(256)} %copy-done.23) | copy-start | bytes 3076
  431.6 93.9 %copy-start.27 = (f32[544]{0:T(1024)S(1)}, f32[544]{0:T(1024)}, u32[]{:S(2)}) copy-start(f32[544]{0:T(1024)} %param.34) | copy-start | bytes 6532
  431.7 127.1 %all-gather.21.cloned.1.call-start = ((), (), s32[]{:S(2)}) async-start(), calls=%async_computation.25 | async-start | bytes 1392640 | tf_op jit(solution)/shard_map/all_gather | solution.py:42
  528.1 40.6 %reduce-scatter.22.cloned.1.call-start = ((), (), s32[]{:S(2)}) async-start(), calls=%async_computation.26 | async-start | bytes 1671168 | tf_op jit(solution)/shard_map/reduce_scatter | solution.py:68
  570.5 14.6 all-to-all-start.2
  585.2 35.9 %reduce-scatter.26.cloned.1.call-start = ((), (), s32[]{:S(2)}) async-start(), calls=%async_computation.30 | async-start | bytes 589824 | tf_op jit(solution)/shard_map/while/body/eval_jaxpr/reduce_scatter | solution.py:268
  622.6 35.0 %reduce-scatter.26.cloned.1.call-start = ((), (), s32[]{:S(2)}) async-start(), calls=%async_computation.30 | async-start | bytes 589824 | tf_op jit(solution)/shard_map/while/body/eval_jaxpr/reduce_scatter | solution.py:268
  659.2 34.9 %reduce-scatter.26.cloned.1.call-start = ((), (), s32[]{:S(2)}) async-start(), calls=%async_computation.30 | async-start | bytes 589824 | tf_op jit(solution)/shard_map/while/body/eval_jaxpr/reduce_scatter | solution.py:268
  695.6 35.0 %reduce-scatter.26.cloned.1.call-start = ((), (), s32[]{:S(2)}) async-start(), calls=%async_computation.30 | async-start | bytes 589824 | tf_op jit(solution)/shard_map/while/body/eval_jaxpr/reduce_scatter | solution.py:268
  732.1 35.0 %reduce-scatter.26.cloned.1.call-start = ((), (), s32[]{:S(2)}) async-start(), calls=%async_computation.30 | async-start | bytes 589824 | tf_op jit(solution)/shard_map/while/body/eval_jaxpr/reduce_scatter | solution.py:268
  768.6 34.9 %reduce-scatter.26.cloned.1.call-start = ((), (), s32[]{:S(2)}) async-start(), calls=%async_computation.30 | async-start | bytes 589824 | tf_op jit(solution)/shard_map/while/body/eval_jaxpr/reduce_scatter | solution.py:268
  805.1 34.9 %reduce-scatter.26.cloned.1.call-start = ((), (), s32[]{:S(2)}) async-start(), calls=%async_computation.30 | async-start | bytes 589824 | tf_op jit(solution)/shard_map/while/body/eval_jaxpr/reduce_scatter | solution.py:268
  841.5 34.9 %reduce-scatter.26.cloned.1.call-start = ((), (), s32[]{:S(2)}) async-start(), calls=%async_computation.30 | async-start | bytes 589824 | tf_op jit(solution)/shard_map/while/body/eval_jaxpr/reduce_scatter | solution.py:268
  878.0 34.9 %reduce-scatter.26.cloned.1.call-start = ((), (), s32[]{:S(2)}) async-start(), calls=%async_computation.30 | async-start | bytes 589824 | tf_op jit(solution)/shard_map/while/body/eval_jaxpr/reduce_scatter | solution.py:268
  914.4 35.0 %reduce-scatter.26.cloned.1.call-start = ((), (), s32[]{:S(2)}) async-start(), calls=%async_computation.30 | async-start | bytes 589824 | tf_op jit(solution)/shard_map/while/body/eval_jaxpr/reduce_scatter | solution.py:268
  950.9 35.0 %reduce-scatter.26.cloned.1.call-start = ((), (), s32[]{:S(2)}) async-start(), calls=%async_computation.30 | async-start | bytes 589824 | tf_op jit(solution)/shard_map/while/body/eval_jaxpr/reduce_scatter | solution.py:268
  987.4 35.0 %reduce-scatter.26.cloned.1.call-start = ((), (), s32[]{:S(2)}) async-start(), calls=%async_computation.30 | async-start | bytes 589824 | tf_op jit(solution)/shard_map/while/body/eval_jaxpr/reduce_scatter | solution.py:268
  1024.0 35.0 %reduce-scatter.26.cloned.1.call-start = ((), (), s32[]{:S(2)}) async-start(), calls=%async_computation.30 | async-start | bytes 589824 | tf_op jit(solution)/shard_map/while/body/eval_jaxpr/reduce_scatter | solution.py:268
  1060.5 34.9 %reduce-scatter.26.cloned.1.call-start = ((), (), s32[]{:S(2)}) async-start(), calls=%async_computation.30 | async-start | bytes 589824 | tf_op jit(solution)/shard_map/while/body/eval_jaxpr/reduce_scatter | solution.py:268
  1096.9 35.0 %reduce-scatter.26.cloned.1.call-start = ((), (), s32[]{:S(2)}) async-start(), calls=%async_computation.30 | async-start | bytes 589824 | tf_op jit(solution)/shard_map/while/body/eval_jaxpr/reduce_scatter | solution.py:268
  1133.5 34.9 %reduce-scatter.26.cloned.1.call-start = ((), (), s32[]{:S(2)}) async-start(), calls=%async_computation.30 | async-start | bytes 589824 | tf_op jit(solution)/shard_map/while/body/eval_jaxpr/reduce_scatter | solution.py:268
  1169.9 35.0 %reduce-scatter.26.cloned.1.call-start = ((), (), s32[]{:S(2)}) async-start(), calls=%async_computation.30 | async-start | bytes 589824 | tf_op jit(solution)/shard_map/while/body/eval_jaxpr/reduce_scatter | solution.py:268
  1206.5 33.5 %all-gather.23.cloned.1.call-start = ((), (), s32[]{:S(2)}) async-start(), calls=%async_computation.27 | async-start | bytes 2506752 | tf_op jit(solution)/shard_map/all_gather | solution.py:46
  1230.7 60.8 %reduce-scatter.24.cloned.1.call-start = ((), (), s32[]{:S(2)}) async-start(), calls=%async_computation.28 | async-start | bytes 2785280 | tf_op jit(solution)/shard_map/reduce_scatter | solution.py:83
  1244.1 214.8 %all-reduce.8.cloned.1.call-start = ((), (), s32[]{:S(2)}) async-start(), calls=%async_computation.29 | async-start | bytes 15319040 | tf_op jit(solution)/shard_map/psum | solution.py:303
  1256.9 34.6 %copy-start.12 = (f32[544]{0:T(1024)S(1)}, f32[544]{0:T(1024)}, u32[]{:S(2)}) copy-start(f32[544]{0:T(1024)} %param.22) | copy-start | bytes 6532
  1256.9 34.6 %copy-start.15 = (f32[256,1]{0,1:T(1,128)S(1)}, f32[256,1]{0,1:T(1,128)}, u32[]{:S(2)}) copy-start(f32[256,1]{0,1:T(1,128)} %copy-done.14) | copy-start | bytes 3076
  1256.9 86.2 %copy-start.7 = (f32[256,544]{0,1:T(8,128)S(1)}, f32[256,544]{0,1:T(8,128)}, u32[]{:S(2)}) copy-start(f32[256,544]{0,1:T(8,128)} %get-tuple-element.602) | copy-start | bytes 1671172
  (30 other events, 302.4 us)
Sparse Core Ops, SparseCore 0:
  13.0 33.6 all-gather.8
  51.6 9.4 reduce-scatter.9
  90.1 48.9 all-gather.10
  256.7 45.0 reduce-scatter.11
  303.8 30.4 all-gather.16
  336.4 29.3 all-gather.12
  368.2 10.5 reduce-scatter.17
  381.2 13.6 reduce-scatter.13
  401.0 11.9 all-gather.18
  415.1 11.9 all-gather.14
  430.0 47.1 reduce-scatter.19
  480.1 45.3 reduce-scatter.15
  528.2 30.4 all-gather.20
  561.8 6.9 reduce-scatter.21
  591.1 29.9 reduce-scatter.25
  628.5 29.1 reduce-scatter.25
  665.0 29.0 reduce-scatter.25
  701.5 29.1 reduce-scatter.25
  738.0 29.1 reduce-scatter.25
  774.5 29.0 reduce-scatter.25
  810.9 29.0 reduce-scatter.25
  847.3 29.0 reduce-scatter.25
  883.8 29.0 reduce-scatter.25
  920.3 29.1 reduce-scatter.25
  956.8 29.1 reduce-scatter.25
  993.3 29.1 reduce-scatter.25
  1029.8 29.1 reduce-scatter.25
  1066.3 29.0 reduce-scatter.25
  1102.7 29.1 reduce-scatter.25
  1139.3 29.0 reduce-scatter.25
  1175.7 29.1 reduce-scatter.25
  1230.8 9.1 all-gather.22
  1244.2 47.1 reduce-scatter.23
  1296.5 162.4 all-reduce.7
where the time goes:
time: 1480 us; the launch traced here: 1470 us
  waiting for transfers between devices  994 us (67%)
  matrix products  184 us (12%)
  blocking collectives  117 us (8%)
  local copies, waits for them, and re-layouts  108 us (7%)
  other arithmetic  47.9 us (3%)
  between operations  16 us (1%)
    reduce_scatter x17, waiting for transfers between devices, backward_head(): lax.psum_scatter(jnp.concatenate([key_part, value_part], axis=1), ('row',...  475 us
    reduce_scatter x4, waiting for transfers between devices, scatter_rows(): lax.psum_scatter(partial_term(jnp.int32(0), lax.axis_size('row') * (opera...  165 us
    all_gather x4, waiting for transfers between devices, gather_rows(): return lax.all_gather(payload, 'row', axis=0, tiled=True)  115 us
    psum x1, waiting for transfers between devices, on_device(): lax.psum((qkv_grad, out_grad, up_grad, down_grad), 'dp')  114 us
    dot_general x34, matrix products, masked_scores(): lax.dot_general(query_head, key_head, (((1,), (1,)), ((), ())), preferred...  48.5 us
    all_gather x1, waiting for transfers between devices, on_device(): all_keys = lax.all_gather(key_value, ('row', 'col'), axis=0, tiled=True)  45.6 us
    psum x1, blocking collectives, on_device(): lax.psum((place_part(first_gain_part, col_index, D), place_part(first_shi...  42.4 us
    reduce_scatter x4, waiting for transfers between devices, scatter_cols(): lax.psum_scatter(partial_term(jnp.int32(0), lax.axis_size('col') * (opera...  39.4 us
  transfers between devices with their start and end apart: 35, of which 35 were waited for; matrix products, arithmetic and copies ran while one was open for 5% of the time, Pallas kernels for 0%

commit v1 on v0

v1 whole, which is shorter than its diff:
```python
import functools

import jax
import jax.numpy as jnp
import numpy as np
from jax import lax
from jax.experimental import pallas as pl
from jax.experimental.pallas import tpu as pltpu
from jax.sharding import PartitionSpec as P

D = 1088
HEADS = 17
HEAD_DIM = 64
FF = 4352
TOK_G = 1024

EPSILON = 1e-05
MASKED = -1e30
CHUNK = 256
BF16 = jnp.bfloat16
F32 = jnp.float32


def swap(payload, axis, distance):
    size = lax.axis_size(axis)
    return lax.ppermute(payload, axis, [(i, i ^ distance) for i in range(size)])


def gather_blocks(payload, axis):
    return [payload] + [swap(payload, axis, k) for k in range(1, lax.axis_size(axis))]


def send_blocks(blocks, axis):
    return [blocks[0]] + [swap(blocks[k], axis, k) for k in range(1, len(blocks))]


def scatter_sum(blocks, axis):
    received = [swap(blocks[k].astype(BF16), axis, k) for k in range(1, len(blocks))]
    total = blocks[0]
    for item in received:
        total = total + item.astype(F32)
    return total


def rows_of(matrix, parts):
    size = matrix.shape[0] // parts
    return [matrix[k * size : (k + 1) * size] for k in range(parts)]


def head_starts(rows):
    return [int(np.floor(HEADS * r / rows + 0.5)) for r in range(rows + 1)]


def most_heads(rows):
    starts = head_starts(rows)
    return max(b - a for a, b in zip(starts[:-1], starts[1:]))


def window_columns(rows, copies):
    starts = head_starts(rows)
    width = most_heads(rows) * HEAD_DIM
    table = np.full((rows, copies * width), -1, np.int64)
    for r in range(rows):
        count = (starts[r + 1] - starts[r]) * HEAD_DIM
        for t in range(copies):
            table[r, t * width : t * width + count] = t * D + starts[r] * HEAD_DIM + np.arange(count)
    return table


def move_tables(rows, copies):
    windows = window_columns(rows, copies)
    shard = copies * D // rows
    moves = []
    for k in range(rows):
        places, columns = [], []
        for r in range(rows):
            place = [p for p in range(windows.shape[1]) if windows[r, p] >= 0 and windows[r, p] // shard == r ^ k]
            places.append(place)
            columns.append([int(windows[r, p] % shard) for p in place])
        longest = max(len(place) for place in places)
        if longest == 0:
            continue
        longest = -(-longest // 16) * 16
        at = np.full((rows, longest), -1, np.int32)
        frm = np.full((rows, longest), -1, np.int32)
        for r in range(rows):
            at[r, : len(places[r])] = places[r]
            frm[r ^ k, : len(columns[r])] = columns[r]
        moves.append((k, at, frm))
    return moves, windows.shape[1], shard


def one_hot(table, row_index, size):
    chosen = lax.dynamic_index_in_dim(jnp.asarray(table), row_index, 0, keepdims=True)
    return (lax.broadcasted_iota(jnp.int32, (size, table.shape[1]), 0) == chosen).astype(BF16)


def mm(a, b):
    return jnp.dot(a, b, preferred_element_type=F32)


def mm_nt(a, b):
    return lax.dot_general(a, b, (((1,), (1,)), ((), ())), preferred_element_type=F32)


def mm_tn(a, b):
    return lax.dot_general(a, b, (((0,), (0,)), ((), ())), preferred_element_type=F32)


def to_window(matrix, moves, window, shard, row_index):
    total = 0.0
    for k, at, frm in moves:
        if k == 0:
            pick = mm_nt(one_hot(frm, row_index, shard), one_hot(at, row_index, window)).astype(BF16)
            total = total + mm(matrix, pick)
        else:
            slab = swap(mm(matrix, one_hot(frm, row_index, shard)).astype(BF16), "row", k)
            total = total + mm_nt(slab, one_hot(at, row_index, window))
    return total.astype(BF16)


def from_window(matrix, moves, window, shard, row_index):
    total = 0.0
    for k, at, frm in moves:
        if k == 0:
            pick = mm_nt(one_hot(at, row_index, window), one_hot(frm, row_index, shard)).astype(BF16)
            total = total + mm(matrix, pick)
        else:
            slab = swap(mm(matrix, one_hot(at, row_index, window)).astype(BF16), "row", k)
            total = total + mm_nt(slab, one_hot(frm, row_index, shard))
    return total.astype(BF16)


def positions(start, shape, dim, block, col):
    at = lax.broadcasted_iota(jnp.int32, shape, dim) + start
    shift = block.bit_length() - 1
    return lax.shift_left(lax.shift_right_logical(at, shift), shift + 1) + (at & (block - 1)) + col * block


def segments(pos, scal_ref):
    first = scal_ref[2]
    return (pos >= first).astype(jnp.int32) + (pos >= first + scal_ref[3]).astype(jnp.int32)


def mask_bias(scal_ref, query_at, query_shape, query_dim, key_shape, key_dim, block, key_col):
    query_pos = positions(query_at, query_shape, query_dim, block, scal_ref[1])
    key_pos = positions(0, key_shape, key_dim, block, key_col)
    allowed = (key_pos <= query_pos) & (segments(key_pos, scal_ref) == segments(query_pos, scal_ref))
    return jnp.where(allowed, 0.0, MASKED)


def in_order(source_ref, target_ref, row, blocks, block):
    for j in range(blocks):
        target_ref[j * block : (j + 1) * block, :] = source_ref[j ^ row]


def forward_kernel(blocks, block, heads, scal_ref, q_ref, kv0_ref, kv1_ref, out_ref, lse_ref, q_s, kv0_s, kv1_s, o_s):
    row = scal_ref[0]
    width = heads * HEAD_DIM
    in_order(q_ref, q_s, row, blocks, block)
    in_order(kv0_ref, kv0_s, row, blocks, block)
    in_order(kv1_ref, kv1_s, row, blocks, block)
    own = scal_ref[1]
    for i in range(blocks * block // CHUNK):
        span = slice(i * CHUNK, (i + 1) * CHUNK)
        keys = (i + 1) * CHUNK
        shape = (CHUNK, keys)
        bias0 = mask_bias(scal_ref, i * CHUNK, (CHUNK, 1), 0, (1, keys), 1, block, own)
        bias1 = mask_bias(scal_ref, i * CHUNK, (CHUNK, 1), 0, (1, keys), 1, block, 1 - own)
        for h in range(heads):
            at = slice(h * HEAD_DIM, (h + 1) * HEAD_DIM)
            va = slice(width + h * HEAD_DIM, width + (h + 1) * HEAD_DIM)
            query = q_s[span, at]
            s0 = mm_nt(query, kv0_s[:keys, at]) + bias0
            s1 = mm_nt(query, kv1_s[:keys, at]) + bias1
            top = jnp.maximum(jnp.max(s0, axis=1, keepdims=True), jnp.max(s1, axis=1, keepdims=True))
            e0 = jnp.exp(s0 - top)
            e1 = jnp.exp(s1 - top)
            total = jnp.sum(e0, axis=1, keepdims=True) + jnp.sum(e1, axis=1, keepdims=True)
            result = mm(e0.astype(BF16), kv0_s[:keys, va]) + mm(e1.astype(BF16), kv1_s[:keys, va])
            o_s[span, at] = (result / total).astype(BF16)
            lse_ref[span, h : h + 1] = top + jnp.log(total)
    for j in range(blocks):
        out_ref[j ^ row] = o_s[j * block : (j + 1) * block, :]


def backward_kernel(
    blocks,
    block,
    heads,
    scal_ref,
    q_ref,
    kv0_ref,
    kv1_ref,
    g_ref,
    lse_ref,
    dq_ref,
    own_ref,
    other_ref,
    q_s,
    kv0_s,
    kv1_s,
    g_s,
    dq_s,
    d0_s,
    d1_s,
):
    row = scal_ref[0]
    width = heads * HEAD_DIM
    in_order(q_ref, q_s, row, blocks, block)
    in_order(kv0_ref, kv0_s, row, blocks, block)
    in_order(kv1_ref, kv1_s, row, blocks, block)
    in_order(g_ref, g_s, row, blocks, block)
    own = scal_ref[1]
    chunks = blocks * block // CHUNK
    for i in reversed(range(chunks)):
        span = slice(i * CHUNK, (i + 1) * CHUNK)
        keys = (i + 1) * CHUNK
        bias0 = mask_bias(scal_ref, i * CHUNK, (1, CHUNK), 1, (keys, 1), 0, block, own)
        bias1 = mask_bias(scal_ref, i * CHUNK, (1, CHUNK), 1, (keys, 1), 0, block, 1 - own)
        for h in range(heads):
            at = slice(h * HEAD_DIM, (h + 1) * HEAD_DIM)
            va = slice(width + h * HEAD_DIM, width + (h + 1) * HEAD_DIM)
            query = q_s[span, at]
            grad = g_s[span, at]
            lse = lse_ref[h : h + 1, span]
            p0 = jnp.exp(mm_nt(kv0_s[:keys, at], query) + bias0 - lse)
            p1 = jnp.exp(mm_nt(kv1_s[:keys, at], query) + bias1 - lse)
            dp0 = mm_nt(kv0_s[:keys, va], grad)
            dp1 = mm_nt(kv1_s[:keys, va], grad)
            delta = jnp.sum(p0 * dp0, axis=0, keepdims=True) + jnp.sum(p1 * dp1, axis=0, keepdims=True)
            ds0 = (p0 * (dp0 - delta)).astype(BF16)
            ds1 = (p1 * (dp1 - delta)).astype(BF16)
            if i == chunks - 1:
                d0_s[:keys, at] = mm(ds0, query)
                d1_s[:keys, at] = mm(ds1, query)
                d0_s[:keys, va] = mm(p0.astype(BF16), grad)
                d1_s[:keys, va] = mm(p1.astype(BF16), grad)
            else:
                d0_s[:keys, at] += mm(ds0, query)
                d1_s[:keys, at] += mm(ds1, query)
                d0_s[:keys, va] += mm(p0.astype(BF16), grad)
                d1_s[:keys, va] += mm(p1.astype(BF16), grad)
            dquery = mm_tn(ds0, kv0_s[:keys, at]) + mm_tn(ds1, kv1_s[:keys, at])
            dq_s[span, at] = (dquery * HEAD_DIM ** (-0.5)).astype(BF16)
    for j in range(blocks):
        piece = slice(j * block, (j + 1) * block)
        dq_ref[j ^ row] = dq_s[piece, :]
        own_ref[j ^ row] = d0_s[piece, :]
        other_ref[j ^ row] = d1_s[piece, :].astype(BF16)


def vmem():
    return pl.BlockSpec(memory_space=pltpu.VMEM)


def smem():
    return pl.BlockSpec(memory_space=pltpu.SMEM)


def attend_forward(scal, queries, kv_own, kv_other, heads):
    blocks, block, width = queries.shape
    tokens = blocks * block
    return pl.pallas_call(
        functools.partial(forward_kernel, blocks, block, heads),
        out_shape=(
            jax.ShapeDtypeStruct((blocks, block, width), BF16),
            jax.ShapeDtypeStruct((tokens, heads), F32),
        ),
        in_specs=[smem(), vmem(), vmem(), vmem()],
        out_specs=(vmem(), vmem()),
        scratch_shapes=[
            pltpu.VMEM((tokens, width), BF16),
            pltpu.VMEM((tokens, 2 * width), BF16),
            pltpu.VMEM((tokens, 2 * width), BF16),
            pltpu.VMEM((tokens, width), BF16),
        ],
        compiler_params=pltpu.CompilerParams(vmem_limit_bytes=40 * 2**20),
        cost_estimate=pl.CostEstimate(
            flops=4 * tokens * 3 * tokens // 2 * width, bytes_accessed=6 * tokens * width * 2, transcendentals=heads * tokens * tokens
        ),
        name="attend_forward",
    )(scal, queries, kv_own, kv_other)


def attend_backward(scal, queries, kv_own, kv_other, grads, lse, heads):
    blocks, block, width = queries.shape
    tokens = blocks * block
    return pl.pallas_call(
        functools.partial(backward_kernel, blocks, block, heads),
        out_shape=(
            jax.ShapeDtypeStruct((blocks, block, width), BF16),
            jax.ShapeDtypeStruct((blocks, block, 2 * width), F32),
            jax.ShapeDtypeStruct((blocks, block, 2 * width), BF16),
        ),
        in_specs=[smem(), vmem(), vmem(), vmem(), vmem(), vmem()],
        out_specs=(vmem(), vmem(), vmem()),
        scratch_shapes=[
            pltpu.VMEM((tokens, width), BF16),
            pltpu.VMEM((tokens, 2 * width), BF16),
            pltpu.VMEM((tokens, 2 * width), BF16),
            pltpu.VMEM((tokens, width), BF16),
            pltpu.VMEM((tokens, width), BF16),
            pltpu.VMEM((tokens, 2 * width), F32),
            pltpu.VMEM((tokens, 2 * width), F32),
        ],
        compiler_params=pltpu.CompilerParams(vmem_limit_bytes=44 * 2**20),
        cost_estimate=pl.CostEstimate(
            flops=10 * tokens * 3 * tokens // 2 * width, bytes_accessed=14 * tokens * width * 2, transcendentals=heads * tokens * tokens
        ),
        name="attend_backward",
    )(scal, queries, kv_own, kv_other, grads, lse)


def norm_parts(resid_in):
    mean_value = jnp.sum(resid_in, axis=1, keepdims=True) / D
    square = jnp.sum(resid_in * resid_in, axis=1, keepdims=True) / D
    inverse = lax.rsqrt(square - mean_value * mean_value + EPSILON)
    return ((resid_in - mean_value) * inverse, inverse)


def norm_back(grad_in, normal, inverse, norm_gain):
    scaled = grad_in * norm_gain
    mean_scaled = jnp.sum(scaled, axis=1, keepdims=True) / D
    mean_cross = jnp.sum(scaled * normal, axis=1, keepdims=True) / D
    return inverse * (scaled - mean_scaled - normal * mean_cross)


def gelu_tanh(pre_value):
    return jax.nn.gelu(pre_value, approximate=True)


def on_device(
    tokens,
    lengths,
    first_gain,
    first_shift,
    qkv_weight,
    query_bias,
    value_bias,
    out_weight,
    out_bias,
    second_gain,
    second_shift,
    up_weight,
    up_bias,
    down_weight,
    down_bias,
    cotangent,
):
    rows = lax.axis_size("row")
    row = lax.axis_index("row")
    col = lax.axis_index("col")
    half = tokens.shape[1]
    block = tokens.shape[0] // 2
    heads = most_heads(rows)
    width = heads * HEAD_DIM

    def halves(matrix):
        pair = matrix.reshape(2, block, half)
        mine = lax.dynamic_index_in_dim(pair, col, 0, keepdims=False)
        other = lax.dynamic_index_in_dim(pair, 1 - col, 0, keepdims=False)
        return jnp.concatenate([mine, swap(other, "col", 1)], axis=1)

    def unhalves(matrix):
        mine = matrix[:, :half]
        other = swap(matrix[:, half:], "col", 1)
        return jnp.concatenate([jnp.where(col == 0, mine, other), jnp.where(col == 0, other, mine)], axis=0)

    x_own = halves(tokens)
    x_all = jnp.concatenate(gather_blocks(x_own, "row"), axis=0).astype(F32)

    vectors = jnp.stack([first_gain, first_shift, out_bias, second_gain, second_shift, down_bias])
    vectors = jnp.concatenate([vectors, swap(vectors, "col", 1)], axis=1)
    gain1, shift1, out_b, gain2, shift2, down_b = [vectors[i] for i in range(6)]

    qkv_moves = move_tables(rows, 3)
    out_moves = move_tables(rows, 1)
    qkv_head = to_window(qkv_weight, *qkv_moves, row)
    w_qkv = jnp.concatenate([qkv_head, swap(qkv_head, "col", 1)], axis=0)

    starts = jnp.asarray(np.array(head_starts(rows), np.int32))
    head_at = starts[row] * HEAD_DIM
    live_cols = jnp.arange(width, dtype=jnp.int32) < (starts[row + 1] - starts[row]) * HEAD_DIM

    def bias_window(vector):
        padded = jnp.concatenate([vector, jnp.zeros((width,), F32)])
        return jnp.where(live_cols, lax.dynamic_slice_in_dim(padded, head_at, width), 0.0)

    normal1, inverse1 = norm_parts(x_all)
    normed1 = (normal1 * gain1 + shift1).astype(BF16)
    qkv = mm(normed1, w_qkv)
    queries = (qkv[:, :width] + bias_window(query_bias)).astype(BF16) * BF16(HEAD_DIM ** (-0.5))
    bias_kv = jnp.concatenate([jnp.zeros((width,), F32), bias_window(value_bias)])
    kv_own = (qkv[:, width:] + bias_kv).astype(BF16)
    kv_other = swap(kv_own, "col", 1)
    queries = queries.reshape(rows, block, width)
    kv_own = kv_own.reshape(rows, block, 2 * width)
    kv_other = kv_other.reshape(rows, block, 2 * width)
    scal = jnp.stack([row.astype(jnp.int32), col.astype(jnp.int32), lengths[0, 0], lengths[0, 1]])
    attention, lse = attend_forward(scal, queries, kv_own, kv_other, heads)

    att_own = jnp.concatenate(send_blocks([attention[k] for k in range(rows)], "row"), axis=1)
    out_window = to_window(out_weight.T, *out_moves, row).T
    out_all = jnp.concatenate(gather_blocks(out_window, "row"), axis=0)
    w_out = jnp.concatenate([out_all, swap(out_all, "col", 1)], axis=1)
    resid_mid = x_own.astype(F32) + (mm(att_own, w_out) + out_b)

    normal2, inverse2 = norm_parts(resid_mid)
    normed2 = (normal2 * gain2 + shift2).astype(BF16)
    mlp_in = jnp.concatenate(gather_blocks(normed2, "row"), axis=0)
    w_up = jnp.concatenate([up_weight, swap(up_weight, "col", 1)], axis=0)
    w_down = jnp.concatenate([down_weight, swap(down_weight, "col", 1)], axis=1)

    cot_own = halves(cotangent)
    own_pos = (row * 2 + col) * block + jnp.arange(block, dtype=jnp.int32)
    live = own_pos < lengths[0, 0] + lengths[0, 1]
    grad_out = jnp.where(live[:, None], cot_own, 0.0)
    grad_out_low = grad_out.astype(BF16)
    g_all = jnp.concatenate(gather_blocks(grad_out_low, "row"), axis=0)
    down_bias_part = jnp.sum(grad_out_low.astype(F32), axis=0)

    pre_act = mm(mlp_in, w_up) + up_bias
    act, gelu_back = jax.vjp(gelu_tanh, pre_act)
    act = act.astype(BF16)
    grad_act = mm_nt(g_all, w_down)
    grad_pre = gelu_back(grad_act)[0].astype(BF16)
    up_bias_part = jnp.sum(grad_pre.astype(F32), axis=0)
    grad_normed2 = scatter_sum(rows_of(mm_nt(grad_pre, w_up), rows), "row")
    second_gain_part = jnp.sum(grad_normed2 * normal2, axis=0)
    second_shift_part = jnp.sum(grad_normed2, axis=0)
    grad_mid = grad_out + norm_back(grad_normed2, normal2, inverse2, gain2)
    grad_mid_low = grad_mid.astype(BF16)
    out_bias_part = jnp.sum(grad_mid_low.astype(F32), axis=0)

    grad_att = mm_nt(grad_mid_low, w_out).astype(BF16)
    grad_att = jnp.stack(send_blocks([grad_att[:, k * width : (k + 1) * width] for k in range(rows)], "row"))
    mid_all = jnp.concatenate(gather_blocks(grad_mid_low, "row"), axis=0)

    block_out = scatter_sum(rows_of(mm(act, w_down), rows), "row")
    block_out = unhalves((resid_mid + (block_out + down_b)).astype(BF16))

    def over_cols(matrix, axis):
        mine, other = jnp.split(matrix, 2, axis=axis)
        return (mine + swap(other.astype(BF16), "col", 1).astype(F32)).astype(BF16)

    down_grad = over_cols(mm_tn(act, g_all), 1)
    up_grad = over_cols(mm_tn(mlp_in, grad_pre), 0)
    out_grad = over_cols(mm_tn(attention.reshape(-1, width), mid_all), 1)
    out_grad = from_window(out_grad.T, *out_moves, row).T
    up_grad, down_grad, out_grad = [g.astype(F32) for g in lax.psum((up_grad, down_grad, out_grad), "dp")]

    dq, dkv_own, dkv_other = attend_backward(scal, queries, kv_own, kv_other, grad_att, lse.T, heads)
    dkv = (dkv_own + swap(dkv_other, "col", 1).astype(F32)).astype(BF16)
    grad_qkv = jnp.concatenate([dq, dkv], axis=2).reshape(-1, 3 * width)
    qkv_bias_part = jnp.sum(grad_qkv.astype(F32), axis=0)
    normed_part = mm_nt(grad_qkv, w_qkv)
    first_gain_part = jnp.sum(normed_part * normal1, axis=0)
    first_shift_part = jnp.sum(normed_part, axis=0)
    grad_normed1 = scatter_sum(rows_of(normed_part, rows), "row")
    back1 = norm_back(grad_normed1, normal1[:block], inverse1[:block], gain1)
    input_grad = unhalves(grad_mid + back1)

    qkv_grad = over_cols(mm_tn(normed1, grad_qkv), 0)
    qkv_grad = from_window(qkv_grad, *qkv_moves, row)
    qkv_grad = lax.psum(qkv_grad, "dp").astype(F32)

    def place(vector):
        mine, other = vector[:half], vector[half:]
        return jnp.concatenate([jnp.where(col == 0, mine, other), jnp.where(col == 0, other, mine)])

    def place_window(vector):
        padded = lax.dynamic_update_slice_in_dim(jnp.zeros((D + width,), F32), vector, head_at, 0)
        return padded[:D]

    def place_rows(vector):
        return lax.dynamic_update_slice_in_dim(jnp.zeros((FF,), F32), vector, row * vector.shape[0], 0)

    every = ("dp", "row", "col")
    early = lax.psum(
        jnp.concatenate(
            [
                place_rows(up_bias_part),
                place(down_bias_part),
                place(second_gain_part),
                place(second_shift_part),
                place(out_bias_part),
            ]
        ),
        every,
    )
    late = lax.psum(
        jnp.concatenate(
            [
                place(first_gain_part),
                place(first_shift_part),
                place_window(qkv_bias_part[:width]),
                place_window(qkv_bias_part[2 * width :]),
            ]
        ),
        every,
    )

    def own_half(vector, at):
        return lax.dynamic_slice_in_dim(vector, at + col * half, half)

    up_width = up_bias.shape[0]
    return (
        block_out,
        input_grad,
        own_half(late, 0),
        own_half(late, D),
        qkv_grad,
        late[2 * D : 3 * D],
        late[3 * D :],
        out_grad,
        own_half(early, FF + 3 * D),
        own_half(early, FF + D),
        own_half(early, FF + 2 * D),
        up_grad,
        lax.dynamic_slice_in_dim(early, row * up_width, up_width),
        down_grad,
        own_half(early, FF),
    )


def solution(mesh):
    in_specs = (
        P(("dp", "row"), "col"),
        P("dp", None),
        P("col"),
        P("col"),
        P("col", "row"),
        P(),
        P(),
        P("row", "col"),
        P("col"),
        P("col"),
        P("col"),
        P("col", "row"),
        P("row"),
        P("row", "col"),
        P("col"),
        P(("dp", "row"), "col"),
    )
    out_specs = (
        P(("dp", "row"), "col"),
        P(("dp", "row"), "col"),
        P("col"),
        P("col"),
        P("col", "row"),
        P(),
        P(),
        P("row", "col"),
        P("col"),
        P("col"),
        P("col"),
        P("col", "row"),
        P("row"),
        P("row", "col"),
        P("col"),
    )
    return jax.shard_map(
        on_device, mesh=mesh, in_specs=in_specs, out_specs=out_specs, check_vma=False
    )
```

time: 1480 us -> 525 us (0.35)
  waiting for transfers between devices: 994 us -> 156 us
  starting transfers between devices: 6.02 us -> 106 us
  matrix products: 184 us -> 85.9 us
  blocking collectives: 117 us -> 44.1 us
  local copies, waits for them, and re-layouts: 108 us -> 55 us
    reduce_scatter x25 -> x0, waiting for transfers between devices: 679 us -> none  [the longest x17 475 us: backward_head(): lax.psum_scatter(jnp.concatenate([key_part, value_part], axis=1), ('row',...]
    all_gather x8 -> x0, waiting for transfers between devices: 190 us -> none  [the longest x4 115 us: gather_rows(): return lax.all_gather(payload, 'row', axis=0, tiled=True)]
    ppermute x0 -> x55, waiting for transfers between devices: none -> 112 us  [swap(): return lax.ppermute(payload, axis, [(i, i ^ distance) for i in range(size)])]
    ppermute x0 -> x55, starting transfers between devices: none -> 106 us  [swap(): return lax.ppermute(payload, axis, [(i, i ^ distance) for i in range(size)])]
    dot_general x131 -> x36, matrix products: 184 us -> 85.9 us  [the longest x14 36 us: mm_nt(): lax.dot_general(a, b, (((1,), (1,)), ((), ())), preferred_element_type=F32)]
    dynamic_update_slice x75 -> x3, local copies, waits for them, and re-layouts: 71.5 us -> 0.47 us  [the longest x1 0.26 us: place_rows(): lax.dynamic_update_slice_in_dim(jnp.zeros((FF,), F32), vector, row * vect...]
    psum x1, waiting for transfers between devices: 114 us -> 44.1 us  [on_device(): qkv_grad = lax.psum(qkv_grad, 'dp').astype(F32)]
    all_to_all x3 -> x0, blocking collectives: 61.7 us -> none  [the longest x2 35.4 us: from_heads(): lax.all_to_all(payload, 'row', split_axis=1, concat_axis=0, tiled=True)]
  transfers between devices with their start and end apart: 35 -> 56, of which waited for: 35 -> 17; matrix products, arithmetic and copies ran while one was open for 5% -> 26% of each run, Pallas kernels for 0% -> 3%
where the time goes in v1:
time: 525 us; the launch traced here: 515 us
  waiting for transfers between devices  156 us (30%)
  starting transfers between devices  106 us (20%)
  matrix products  85.9 us (16%)
  local copies, waits for them, and re-layouts  55 us (10%)
  blocking collectives  44.1 us (8%)
  other arithmetic  35.5 us (7%)
  between operations  18.8 us (4%)
  Pallas kernels  14.7 us (3%)
    ppermute x55, waiting for transfers between devices, swap(): return lax.ppermute(payload, axis, [(i, i ^ distance) for i in range(size)])  112 us
    ppermute x55, starting transfers between devices, swap(): return lax.ppermute(payload, axis, [(i, i ^ distance) for i in range(size)])  106 us
    psum x1, blocking collectives, on_device(): lax.psum(jnp.concatenate([place(first_gain_part), place(first_shift_part)...  44.1 us
    psum x1, waiting for transfers between devices, on_device(): qkv_grad = lax.psum(qkv_grad, 'dp').astype(F32)  44.1 us
    dot_general x14, matrix products, mm_nt(): lax.dot_general(a, b, (((1,), (1,)), ((), ())), preferred_element_type=F32)  36 us
    dot_general x18, matrix products, mm(): return jnp.dot(a, b, preferred_element_type=F32)  35.7 us
    dot_general x4, matrix products, mm_tn(): lax.dot_general(a, b, (((0,), (0,)), ((), ())), preferred_element_type=F32)  14.2 us
    unnamed x176, local copies, waits for them, and re-layouts  11.1 us
  transfers between devices with their start and end apart: 56, of which 17 were waited for; matrix products, arithmetic and copies ran while one was open for 26% of the time, Pallas kernels for 3%

profile of v1, /device:TPU:0, one launch (start us, length us, event | category | flops | bytes accessed | tf_op | source)
XLA Modules:
  0.0 515.5 jit_solution(1637079249638068194)
XLA Ops:
  9.8 3.1 collective-permute-start.13
  19.6 2.5 collective-permute-start.14
  37.6 2.6 constant_dynamic-update-slice_fusion.3
  45.8 3.6 fusion.33
  55.6 7.2 %collective-permute-done.5 = bf16[544,320]{0,1:T(8,128)(2,1)S(1)} collective-permute-done((bf16[544,320]{0,1:T(8,128)(2,1)}, bf16[544,320]{0,1:T(8,128)(2,1)S(1)}, u32[]{:S(2)}, u32[]{:S(2)}) %collective-permute-start.5) | collective-permute-done | bytes 348192 | tf_op jit(solution)/shard_map/ppermute | solution.py:26
  72.7 7.0 %collective-permute-done.17 = bf16[320,544]{1,0:T(8,128)(2,1)S(1)} collective-permute-done((bf16[320,544]{1,0:T(8,128)(2,1)S(1)}, bf16[320,544]{1,0:T(8,128)(2,1)S(1)}, u32[]{:S(2)}, u32[]{:S(2)}) %collective-permute-start.17) | collective-permute-done | bytes 348192 | tf_op jit(solution)/shard_map/ppermute | solution.py:26
  79.7 17.2 %collective-permute-start.2 = (bf16[128,1088]{0,1:T(8,128)(2,1)}, bf16[128,1088]{0,1:T(8,128)(2,1)S(1)}, u32[]{:S(2)}, u32[]{:S(2)}) collective-permute-start(bf16[128,1088]{0,1:T(8,128)(2,1)} %pad_maximum_fusion.11), channel_id=1, source_target_pairs={{0,4},{2,6},{4,0},{6,2},{1,5},{3,7},{5,1},{7,3},{8,12},{10,14},{12... | collective-permute-start | bytes 835592 | tf_op jit(solution)/shard_map/ppermute | solution.py:26
  97.0 14.3 %collective-permute-done.16 = bf16[320,544]{1,0:T(8,128)(2,1)S(1)} collective-permute-done((bf16[320,544]{1,0:T(8,128)(2,1)S(1)}, bf16[320,544]{1,0:T(8,128)(2,1)S(1)}, u32[]{:S(2)}, u32[]{:S(2)}) %collective-permute-start.16) | collective-permute-done | bytes 348192 | tf_op jit(solution)/shard_map/ppermute | solution.py:26
  114.9 2.3 collective-permute-done.2
  117.3 11.6 %collective-permute-done.1 = bf16[128,1088]{0,1:T(8,128)(2,1)} collective-permute-done((bf16[128,1088]{0,1:T(8,128)(2,1)}, bf16[128,1088]{0,1:T(8,128)(2,1)}, u32[]{:S(2)}, u32[]{:S(2)}) %collective-permute-start.1) | collective-permute-done | bytes 278560 | tf_op jit(solution)/shard_map/ppermute | solution.py:26
  131.0 3.7 fusion.20
  138.7 5.2 %attend_forward.1 = (bf16[4,128,320]{2,1,0:T(8,128)(2,1)S(1)}, f32[512,5]{1,0:T(8,128)S(1)}) custom-call(s32[4]{0:T(128)S(1)} %pad_add_fusion.scal_ref, bf16[4,128,320]{2,1,0:T(8,128)(2,1)S(1)} %bitcast.114, bf16[4,128,640]{2,1,0:T(8,128)(2,1)S(1)} %bitcast.109, bf16[4,128,640]{2,1,0:T(8,128)(2,1)S(1)} %bitcast.111), custom_call_target="tpu_custom_call" | custom-call | flops 503316480 | bytes 1966080 | tf_op jit(solution)/shard_map/attend_forward/pallas_call | solution.py:264
  145.8 2.6 collective-permute-start.10
  148.5 2.4 constant_dynamic-update-slice_fusion.2
  152.4 2.8 copy.60
  156.2 4.1 fusion.136
  160.7 2.5 collective-permute-start.21
  170.2 27.4 %collective-permute-start.29 = (bf16[128,1088]{0,1:T(8,128)(2,1)}, bf16[128,1088]{0,1:T(8,128)(2,1)S(1)}, u32[]{:S(2)}, u32[]{:S(2)}) collective-permute-start(bf16[128,1088]{0,1:T(8,128)(2,1)} %get-tuple-element.53), channel_id=1, source_target_pairs={{0,2},{2,0},{4,6},{6,4},{1,3},{3,1},{5,7},{7,5},{8,10},{10,8},{12,... | collective-permute-start | bytes 835592 | tf_op jit(solution)/shard_map/ppermute | solution.py:26
  197.5 5.6 %collective-permute-done.20 = bf16[128,1088]{0,1:T(8,128)(2,1)} collective-permute-done((bf16[128,1088]{0,1:T(8,128)(2,1)S(1)}, bf16[128,1088]{0,1:T(8,128)(2,1)}, u32[]{:S(2)}, u32[]{:S(2)}) %collective-permute-start.20) | collective-permute-done | bytes 278560 | tf_op jit(solution)/shard_map/ppermute | solution.py:26
  203.1 3.6 convolution_add_fusion
  206.7 3.2 fusion.149
  209.9 4.1 convert_reduce_fusion.1
  214.1 4.7 fusion.148
  226.5 3.1 fusion.95
  230.9 5.4 %fusion.97 = f32[1088,1088]{1,0:T(8,128)} fusion(bf16[512,1088]{0,1:T(8,128)(2,1)S(1)} %get-tuple-element.120, bf16[128,1088]{0,1:T(8,128)(2,1)S(1)} %collective-permute-done.21, bf16[128,1088]{0,1:T(8,128)(2,1)} %collective-permute-done.20, bf16[128,1088]{0,1:T(8,128)(2,1)} %collective-permute-done.19, bf16[128,1088]{0,1:T(8,128)(2,1)S(1)} %add_convert_fusion.3), kind=kOutput, calls=%fused_computation.166 | convolution fusion | flops 1216610304 | bytes 6963200 | tf_op jit(solution)/shard_map/dot_general | solution.py:107
  236.3 2.9 split.61
  240.8 20.0 %collective-permute-done.33 = bf16[128,1088]{0,1:T(8,128)(2,1)} collective-permute-done((bf16[128,1088]{0,1:T(8,128)(2,1)}, bf16[128,1088]{0,1:T(8,128)(2,1)}, u32[]{:S(2)}, u32[]{:S(2)}) %collective-permute-start.33) | collective-permute-done | bytes 278560 | tf_op jit(solution)/shard_map/ppermute | solution.py:26
  262.9 8.6 %collective-permute-done.25 = bf16[128,1088]{0,1:T(8,128)(2,1)S(1)} collective-permute-done((bf16[128,1088]{0,1:T(8,128)(2,1)}, bf16[128,1088]{0,1:T(8,128)(2,1)S(1)}, u32[]{:S(2)}, u32[]{:S(2)}) %collective-permute-start.25) | collective-permute-done | bytes 278560 | tf_op jit(solution)/shard_map/ppermute | solution.py:26
  271.5 2.6 convert_reduce_fusion.3
  275.4 3.0 collective-permute-start.47
  278.6 13.0 %convolution_convert_fusion = bf16[128,1280]{1,0:T(8,128)(2,1)S(1)} fusion(bf16[128,1088]{0,1:T(8,128)(2,1)} %get-tuple-element.50, bf16[1280,544]{1,0:T(8,128)(2,1)S(1)} %copy-done.14, bf16[320,544]{1,0:T(8,128)(2,1)S(1)} %copy-done.39, bf16[320,544]{1,0:T(8,128)(2,1)S(1)} %copy-done.41, bf16[320,544]{1,0:T(8,128)(2,1)S(1)} %copy-done.43, ...), kind=kOutput, calls=%fused_computation.17 | convolution fusion | flops 370606080 | bytes 3391488 | tf_op jit(solution)/shard_map/dot_general | solution.py:103
  293.3 5.5 %collective-permute-done.37 = bf16[128,320]{1,0:T(8,128)(2,1)S(1)} collective-permute-done((bf16[128,320]{1,0:T(8,128)(2,1)S(1)}, bf16[128,320]{1,0:T(8,128)(2,1)S(1)}, u32[]{:S(2)}, u32[]{:S(2)}) %collective-permute-start.37) | collective-permute-done | bytes 81952 | tf_op jit(solution)/shard_map/ppermute | solution.py:26
  298.8 6.9 %collective-permute-start.35 = (bf16[128,320]{1,0:T(8,128)(2,1)S(1)}, bf16[128,320]{1,0:T(8,128)(2,1)S(1)}, u32[]{:S(2)}, u32[]{:S(2)}) collective-permute-start(bf16[128,320]{1,0:T(8,128)(2,1)S(1)} %get-tuple-element.82), channel_id=1, source_target_pairs={{0,2},{2,0},{4,6},{6,4},{1,3},{3,1},{5,7},{7,5},{8,10},{10,8},{12,... | collective-permute-start | bytes 245768 | tf_op jit(solution)/shard_map/ppermute | solution.py:26
  309.4 9.5 %attend_backward.1 = (bf16[4,128,320]{2,1,0:T(8,128)(2,1)S(1)}, f32[4,128,640]{2,1,0:T(8,128)S(1)}, bf16[4,128,640]{2,1,0:T(8,128)(2,1)}) custom-call(s32[4]{0:T(128)S(1)} %pad_add_fusion.scal_ref, bf16[4,128,320]{2,1,0:T(8,128)(2,1)S(1)} %bitcast.115, bf16[4,128,640]{2,1,0:T(8,128)(2,1)S(1)} %bitcast.110, bf16[4,128,640]{2,1,0:T(8,128)(2,1)S(1)} %bitcast.112, ...), custom_call_target="tpu_custom_call" | custom-call | flops 1258291200 | bytes 4587520 | tf_op jit(solution)/shard_map/attend_backward/pallas_call | solution.py:289
  326.4 2.5 collective-permute-start.52
  330.5 4.9 collective-permute-done.52
  340.9 3.8 fusion.132
  348.6 5.9 %fusion.134 = (f32[1088]{0:T(1024)S(1)}, f32[1088]{0:T(1024)S(1)}, bf16[512,1088]{0,1:T(8,128)(2,1)}, f32[512,1088]{0,1:T(8,128)}, f32[512,1088]{0,1:T(8,128)}) fusion(f32[512]{0:T(512)S(1)} %copy-done.75, f32[512]{0:T(512)S(1)} %copy-done.73, bf16[512,1088]{0,1:T(8,128)(2,1)S(1)} %copy-done.28, bf16[512,960]{1,0:T(8,128)(2,1)} %bitcast.123, ...), kind=kOutput, calls=%fused_computation.271 | convolution fusion | flops 1077622784 | bytes 9769472 | tf_op jit(solution)/shard_map/dot_general | solution.py:103
  354.6 3.3 fusion
  357.9 3.3 fusion.1
  367.1 5.0 fusion.35
  375.6 2.4 collective-permute-start.46
  378.1 15.1 %collective-permute-done.45 = bf16[544,304]{1,0:T(8,128)(2,1)S(1)} collective-permute-done((bf16[544,304]{1,0:T(8,128)(2,1)S(1)}, bf16[544,304]{1,0:T(8,128)(2,1)S(1)}, u32[]{:S(2)}, u32[]{:S(2)}) %collective-permute-start.45) | collective-permute-done | bytes 330784 | tf_op jit(solution)/shard_map/ppermute | solution.py:26
  394.0 3.7 collective-permute-done.44
  402.4 2.6 collective-permute-start.41
  405.9 44.1 %all-reduce.3 = (f32[4352]{0:T(1024)S(1)}, f32[8704]{0:T(1024)S(1)}) all-reduce(f32[4352]{0:T(1024)S(1)} %concatenate.81, f32[8704]{0:T(1024)S(1)} %concatenate.83), channel_id=1, replica_groups=mesh['dp'=4,'row'=4,'col'=2] {'dp','row','col'}, use_global_device_ids=true, to_apply=%region_11.12 | all-reduce | flops 13056 | bytes 104448 | tf_op jit(solution)/shard_map/psum | solution.py:492
  456.4 44.1 %all-reduce.7.cloned.1.call-done = (bf16[544,816]{1,0:T(8,128)(2,1)}, bf16[272,544]{1,0:T(8,128)(2,1)}, bf16[544,1088]{1,0:T(8,128)(2,1)}, bf16[1088,544]{0,1:T(8,128)(2,1)}) async-done(((bf16[544,816]{1,0:T(8,128)(2,1)}, bf16[272,544]{1,0:T(8,128)(2,1)}, bf16[544,1088]{1,0:T(8,128)(2,1)}, bf16[1088,544]{0,1:T(8,128)(2,1)}), (bf16[544,816]{1,0:T(8,128)(2,1)}, bf16[272,544]{1,0:T(8,128)(2,1)}, ...) | async-done | bytes 3551248 | tf_op jit(solution)/shard_map/psum | solution.py:466
  502.5 2.6 convert_element_type.275
  (385 shorter events, 129.4 us)
Async XLA Ops:
  7.2 493.3 %all-reduce.7.cloned.1.call-start = ((), (), s32[]{:S(2)}) async-start(), calls=%async_computation | async-start | bytes 7659520 | tf_op jit(solution)/shard_map/psum | solution.py:466
  9.8 41.2 %collective-permute-start.13 = (bf16[544,16]{0,1:T(8,128)(2,1)S(1)}, bf16[544,16]{0,1:T(8,128)(2,1)S(1)}, u32[]{:S(2)}, u32[]{:S(2)}) collective-permute-start(bf16[544,16]{0,1:T(8,128)(2,1)S(1)} %fusion.46), channel_id=1, source_target_pairs={{0,2},{2,0},{4,6},{6,4},{1,3},{3,1},{5,7},{7,5},{8,10},{10,8},{12,... | collective-permute-start | bytes 52232 | tf_op jit(solution)/shard_map/ppermute | solution.py:26
  17.1 51.6 %collective-permute-start.4 = (f32[6,544]{1,0:T(8,128)S(1)}, f32[6,544]{1,0:T(8,128)S(1)}, u32[]{:S(2)}, u32[]{:S(2)}) collective-permute-start(f32[6,544]{1,0:T(8,128)S(1)} %stack.54), channel_id=1, source_target_pairs={{0,1},{1,0},{2,3},{3,2},{4,5},{5,4},{6,7},{7,6},{8,9},{9,8},{10,11... | collective-permute-start | bytes 39176 | tf_op jit(solution)/shard_map/ppermute | solution.py:26
  19.6 45.6 %collective-permute-start.14 = (bf16[544,32]{0,1:T(8,128)(2,1)S(1)}, bf16[544,32]{0,1:T(8,128)(2,1)S(1)}, u32[]{:S(2)}, u32[]{:S(2)}) collective-permute-start(bf16[544,32]{0,1:T(8,128)(2,1)S(1)} %fusion.37), channel_id=1, source_target_pairs={{0,6},{2,4},{4,2},{6,0},{1,7},{3,5},{5,3},{7,1},{8,14},{10,12},{12... | collective-permute-start | bytes 104456 | tf_op jit(solution)/shard_map/ppermute | solution.py:26
  23.3 40.4 %collective-permute-start.7 = (bf16[544,48]{0,1:T(8,128)(2,1)S(1)}, bf16[544,48]{0,1:T(8,128)(2,1)S(1)}, u32[]{:S(2)}, u32[]{:S(2)}) collective-permute-start(bf16[544,48]{0,1:T(8,128)(2,1)S(1)} %fusion.36), channel_id=1, source_target_pairs={{0,6},{2,4},{4,2},{6,0},{1,7},{3,5},{5,3},{7,1},{8,14},{10,12},{12... | collective-permute-start | bytes 156680 | tf_op jit(solution)/shard_map/ppermute | solution.py:26
  27.0 26.6 %collective-permute-start.6 = (bf16[544,304]{0,1:T(8,128)(2,1)}, bf16[544,304]{0,1:T(8,128)(2,1)}, u32[]{:S(2)}, u32[]{:S(2)}) collective-permute-start(bf16[544,304]{0,1:T(8,128)(2,1)} %fusion.32), channel_id=1, source_target_pairs={{0,4},{2,6},{4,0},{6,2},{1,5},{3,7},{5,1},{7,3},{8,12},{10,14},{12... | collective-permute-start | bytes 992264 | tf_op jit(solution)/shard_map/ppermute | solution.py:26
  51.0 11.8 %collective-permute-start.5 = (bf16[544,320]{0,1:T(8,128)(2,1)}, bf16[544,320]{0,1:T(8,128)(2,1)S(1)}, u32[]{:S(2)}, u32[]{:S(2)}) collective-permute-start(bf16[544,320]{0,1:T(8,128)(2,1)} %fusion.31), channel_id=1, source_target_pairs={{0,2},{2,0},{4,6},{6,4},{1,3},{3,1},{5,7},{7,5},{8,10},{10,8},{12,... | collective-permute-start | bytes 1044488 | tf_op jit(solution)/shard_map/ppermute | solution.py:26
  53.6 18.4 %collective-permute-start = (bf16[128,544]{0,1:T(8,128)(2,1)S(1)}, bf16[128,544]{0,1:T(8,128)(2,1)S(1)}, u32[]{:S(2)}, u32[]{:S(2)}) collective-permute-start(bf16[128,544]{0,1:T(8,128)(2,1)S(1)} %bitcast.125), channel_id=1, source_target_pairs={{0,1},{1,0},{2,3},{3,2},{4,5},{5,4},{6,7},{7,6},{8,9},{9,8},{10,11... | collective-permute-start | bytes 417800 | tf_op jit(solution)/shard_map/ppermute | solution.py:26
  65.2 65.8 %collective-permute-start.8 = (bf16[544,960]{1,0:T(8,128)(2,1)}, bf16[544,960]{1,0:T(8,128)(2,1)}, u32[]{:S(2)}, u32[]{:S(2)}) collective-permute-start(bf16[544,960]{1,0:T(8,128)(2,1)} %fusion.14), channel_id=1, source_target_pairs={{0,1},{1,0},{2,3},{3,2},{4,5},{5,4},{6,7},{7,6},{8,9},{9,8},{10,11... | collective-permute-start | bytes 3133448 | tf_op jit(solution)/shard_map/ppermute | solution.py:26
  65.5 14.3 %collective-permute-start.17 = (bf16[320,544]{1,0:T(8,128)(2,1)S(1)}, bf16[320,544]{1,0:T(8,128)(2,1)S(1)}, u32[]{:S(2)}, u32[]{:S(2)}) collective-permute-start(bf16[320,544]{1,0:T(8,128)(2,1)S(1)} %fusion.25), channel_id=1, source_target_pairs={{0,6},{2,4},{4,2},{6,0},{1,7},{3,5},{5,3},{7,1},{8,14},{10,12},{12... | collective-permute-start | bytes 1044488 | tf_op jit(solution)/shard_map/ppermute | solution.py:26
  67.0 44.3 %collective-permute-start.16 = (bf16[320,544]{1,0:T(8,128)(2,1)S(1)}, bf16[320,544]{1,0:T(8,128)(2,1)S(1)}, u32[]{:S(2)}, u32[]{:S(2)}) collective-permute-start(bf16[320,544]{1,0:T(8,128)(2,1)S(1)} %fusion.25), channel_id=1, source_target_pairs={{0,4},{2,6},{4,0},{6,2},{1,5},{3,7},{5,1},{7,3},{8,12},{10,14},{12... | collective-permute-start | bytes 1044488 | tf_op jit(solution)/shard_map/ppermute | solution.py:26
  68.7 42.5 %collective-permute-start.15 = (bf16[320,544]{1,0:T(8,128)(2,1)S(1)}, bf16[320,544]{1,0:T(8,128)(2,1)S(1)}, u32[]{:S(2)}, u32[]{:S(2)}) collective-permute-start(bf16[320,544]{1,0:T(8,128)(2,1)S(1)} %fusion.25), channel_id=1, source_target_pairs={{0,2},{2,0},{4,6},{6,4},{1,3},{3,1},{5,7},{7,5},{8,10},{10,8},{12,... | collective-permute-start | bytes 1044488 | tf_op jit(solution)/shard_map/ppermute | solution.py:26
  72.0 73.8 %collective-permute-start.22 = (bf16[544,1088]{1,0:T(8,128)(2,1)}, bf16[544,1088]{1,0:T(8,128)(2,1)}, u32[]{:S(2)}, u32[]{:S(2)}) collective-permute-start(bf16[544,1088]{1,0:T(8,128)(2,1)} %param.42), channel_id=1, source_target_pairs={{0,1},{1,0},{2,3},{3,2},{4,5},{5,4},{6,7},{7,6},{8,9},{9,8},{10,11... | collective-permute-start | bytes 3551240 | tf_op jit(solution)/shard_map/ppermute | solution.py:26
  79.7 37.5 %collective-permute-start.2 = (bf16[128,1088]{0,1:T(8,128)(2,1)}, bf16[128,1088]{0,1:T(8,128)(2,1)S(1)}, u32[]{:S(2)}, u32[]{:S(2)}) collective-permute-start(bf16[128,1088]{0,1:T(8,128)(2,1)} %pad_maximum_fusion.11), channel_id=1, source_target_pairs={{0,4},{2,6},{4,0},{6,2},{1,5},{3,7},{5,1},{7,3},{8,12},{10,14},{12... | collective-permute-start | bytes 835592 | tf_op jit(solution)/shard_map/ppermute | solution.py:26
  111.3 17.6 %collective-permute-start.1 = (bf16[128,1088]{0,1:T(8,128)(2,1)}, bf16[128,1088]{0,1:T(8,128)(2,1)}, u32[]{:S(2)}, u32[]{:S(2)}) collective-permute-start(bf16[128,1088]{0,1:T(8,128)(2,1)} %pad_maximum_fusion.11), channel_id=1, source_target_pairs={{0,2},{2,0},{4,6},{6,4},{1,3},{3,1},{5,7},{7,5},{8,10},{10,8},{12,... | collective-permute-start | bytes 835592 | tf_op jit(solution)/shard_map/ppermute | solution.py:26
  111.3 17.6 %collective-permute-start.3 = (bf16[128,1088]{0,1:T(8,128)(2,1)}, bf16[128,1088]{0,1:T(8,128)(2,1)}, u32[]{:S(2)}, u32[]{:S(2)}) collective-permute-start(bf16[128,1088]{0,1:T(8,128)(2,1)} %pad_maximum_fusion.11), channel_id=1, source_target_pairs={{0,6},{2,4},{4,2},{6,0},{1,7},{3,5},{5,3},{7,1},{8,14},{10,12},{12... | collective-permute-start | bytes 835592 | tf_op jit(solution)/shard_map/ppermute | solution.py:26
  117.3 47.9 %collective-permute-start.23 = (bf16[1088,544]{0,1:T(8,128)(2,1)}, bf16[1088,544]{0,1:T(8,128)(2,1)}, u32[]{:S(2)}, u32[]{:S(2)}) collective-permute-start(bf16[1088,544]{0,1:T(8,128)(2,1)} %param.44), channel_id=1, source_target_pairs={{0,1},{1,0},{2,3},{3,2},{4,5},{5,4},{6,7},{7,6},{8,9},{9,8},{10,11... | collective-permute-start | bytes 3551240 | tf_op jit(solution)/shard_map/ppermute | solution.py:26
  128.9 22.0 %collective-permute-start.18 = (bf16[1280,544]{0,1:T(8,128)(2,1)}, bf16[1280,544]{0,1:T(8,128)(2,1)}, u32[]{:S(2)}, u32[]{:S(2)}) collective-permute-start(bf16[1280,544]{0,1:T(8,128)(2,1)} %copy.59), channel_id=1, source_target_pairs={{0,1},{1,0},{2,3},{3,2},{4,5},{5,4},{6,7},{7,6},{8,9},{9,8},{10,11... | collective-permute-start | bytes 4177928 | tf_op jit(solution)/shard_map/ppermute | solution.py:26
  144.0 11.1 %collective-permute-start.12 = (bf16[128,320]{1,0:T(8,128)(2,1)S(1)}, bf16[128,320]{1,0:T(8,128)(2,1)S(1)}, u32[]{:S(2)}, u32[]{:S(2)}) collective-permute-start(bf16[128,320]{1,0:T(8,128)(2,1)S(1)} %get-tuple-element.75), channel_id=1, source_target_pairs={{0,6},{2,4},{4,2},{6,0},{1,7},{3,5},{5,3},{7,1},{8,14},{10,12},{12... | collective-permute-start | bytes 245768 | tf_op jit(solution)/shard_map/ppermute | solution.py:26
  145.4 9.9 %collective-permute-start.11 = (bf16[128,320]{1,0:T(8,128)(2,1)S(1)}, bf16[128,320]{1,0:T(8,128)(2,1)S(1)}, u32[]{:S(2)}, u32[]{:S(2)}) collective-permute-start(bf16[128,320]{1,0:T(8,128)(2,1)S(1)} %get-tuple-element.76), channel_id=1, source_target_pairs={{0,4},{2,6},{4,0},{6,2},{1,5},{3,7},{5,1},{7,3},{8,12},{10,14},{12... | collective-permute-start | bytes 245768 | tf_op jit(solution)/shard_map/ppermute | solution.py:26
  145.8 9.5 %collective-permute-start.10 = (bf16[128,320]{1,0:T(8,128)(2,1)S(1)}, bf16[128,320]{1,0:T(8,128)(2,1)S(1)}, u32[]{:S(2)}, u32[]{:S(2)}) collective-permute-start(bf16[128,320]{1,0:T(8,128)(2,1)S(1)} %get-tuple-element.77), channel_id=1, source_target_pairs={{0,2},{2,0},{4,6},{6,4},{1,3},{3,1},{5,7},{7,5},{8,10},{10,8},{12,... | collective-permute-start | bytes 245768 | tf_op jit(solution)/shard_map/ppermute | solution.py:26
  150.9 59.0 %collective-permute-start.31 = (bf16[128,1088]{0,1:T(8,128)(2,1)}, bf16[128,1088]{0,1:T(8,128)(2,1)}, u32[]{:S(2)}, u32[]{:S(2)}) collective-permute-start(bf16[128,1088]{0,1:T(8,128)(2,1)} %get-tuple-element.53), channel_id=1, source_target_pairs={{0,6},{2,4},{4,2},{6,0},{1,7},{3,5},{5,3},{7,1},{8,14},{10,12},{12... | collective-permute-start | bytes 835592 | tf_op jit(solution)/shard_map/ppermute | solution.py:26
  155.1 54.8 %collective-permute-start.30 = (bf16[128,1088]{0,1:T(8,128)(2,1)}, bf16[128,1088]{0,1:T(8,128)(2,1)}, u32[]{:S(2)}, u32[]{:S(2)}) collective-permute-start(bf16[128,1088]{0,1:T(8,128)(2,1)} %get-tuple-element.53), channel_id=1, source_target_pairs={{0,4},{2,6},{4,0},{6,2},{1,5},{3,7},{5,1},{7,3},{8,12},{10,14},{12... | collective-permute-start | bytes 835592 | tf_op jit(solution)/shard_map/ppermute | solution.py:26
  160.7 9.4 %collective-permute-start.21 = (bf16[128,1088]{0,1:T(8,128)(2,1)S(1)}, bf16[128,1088]{0,1:T(8,128)(2,1)S(1)}, u32[]{:S(2)}, u32[]{:S(2)}) collective-permute-start(bf16[128,1088]{0,1:T(8,128)(2,1)S(1)} %add_convert_fusion.3), channel_id=1, source_target_pairs={{0,6},{2,4},{4,2},{6,0},{1,7},{3,5},{5,3},{7,1},{8,14},{10,12},{12... | collective-permute-start | bytes 835592 | tf_op jit(solution)/shard_map/ppermute | solution.py:26
  163.2 39.9 %collective-permute-start.20 = (bf16[128,1088]{0,1:T(8,128)(2,1)S(1)}, bf16[128,1088]{0,1:T(8,128)(2,1)}, u32[]{:S(2)}, u32[]{:S(2)}) collective-permute-start(bf16[128,1088]{0,1:T(8,128)(2,1)S(1)} %add_convert_fusion.3), channel_id=1, source_target_pairs={{0,4},{2,6},{4,0},{6,2},{1,5},{3,7},{5,1},{7,3},{8,12},{10,14},{12... | collective-permute-start | bytes 835592 | tf_op jit(solution)/shard_map/ppermute | solution.py:26
  165.2 37.9 %collective-permute-start.19 = (bf16[128,1088]{0,1:T(8,128)(2,1)S(1)}, bf16[128,1088]{0,1:T(8,128)(2,1)}, u32[]{:S(2)}, u32[]{:S(2)}) collective-permute-start(bf16[128,1088]{0,1:T(8,128)(2,1)S(1)} %add_convert_fusion.3), channel_id=1, source_target_pairs={{0,2},{2,0},{4,6},{6,4},{1,3},{3,1},{5,7},{7,5},{8,10},{10,8},{12,... | collective-permute-start | bytes 835592 | tf_op jit(solution)/shard_map/ppermute | solution.py:26
  170.2 39.8 %collective-permute-start.29 = (bf16[128,1088]{0,1:T(8,128)(2,1)}, bf16[128,1088]{0,1:T(8,128)(2,1)S(1)}, u32[]{:S(2)}, u32[]{:S(2)}) collective-permute-start(bf16[128,1088]{0,1:T(8,128)(2,1)} %get-tuple-element.53), channel_id=1, source_target_pairs={{0,2},{2,0},{4,6},{6,4},{1,3},{3,1},{5,7},{7,5},{8,10},{10,8},{12,... | collective-permute-start | bytes 835592 | tf_op jit(solution)/shard_map/ppermute | solution.py:26
  219.7 19.8 %collective-permute-start.32 = (bf16[128,1088]{0,1:T(8,128)(2,1)}, bf16[128,1088]{0,1:T(8,128)(2,1)}, u32[]{:S(2)}, u32[]{:S(2)}) collective-permute-start(bf16[128,1088]{0,1:T(8,128)(2,1)} %get-tuple-element.62), channel_id=1, source_target_pairs={{0,2},{2,0},{4,6},{6,4},{1,3},{3,1},{5,7},{7,5},{8,10},{10,8},{12,... | collective-permute-start | bytes 835592 | tf_op jit(solution)/shard_map/ppermute | solution.py:26
  219.7 21.1 %collective-permute-start.34 = (bf16[128,1088]{0,1:T(8,128)(2,1)}, bf16[128,1088]{0,1:T(8,128)(2,1)}, u32[]{:S(2)}, u32[]{:S(2)}) collective-permute-start(bf16[128,1088]{0,1:T(8,128)(2,1)} %get-tuple-element.63), channel_id=1, source_target_pairs={{0,6},{2,4},{4,2},{6,0},{1,7},{3,5},{5,3},{7,1},{8,14},{10,12},{12... | collective-permute-start | bytes 835592 | tf_op jit(solution)/shard_map/ppermute | solution.py:26
  221.0 39.8 %collective-permute-start.33 = (bf16[128,1088]{0,1:T(8,128)(2,1)}, bf16[128,1088]{0,1:T(8,128)(2,1)}, u32[]{:S(2)}, u32[]{:S(2)}) collective-permute-start(bf16[128,1088]{0,1:T(8,128)(2,1)} %get-tuple-element.64), channel_id=1, source_target_pairs={{0,4},{2,6},{4,0},{6,2},{1,5},{3,7},{5,1},{7,3},{8,12},{10,14},{12... | collective-permute-start | bytes 835592 | tf_op jit(solution)/shard_map/ppermute | solution.py:26
  224.2 38.6 %collective-permute-start.24 = (bf16[128,1088]{0,1:T(8,128)(2,1)}, bf16[128,1088]{0,1:T(8,128)(2,1)S(1)}, u32[]{:S(2)}, u32[]{:S(2)}) collective-permute-start(bf16[128,1088]{0,1:T(8,128)(2,1)} %get-tuple-element.65), channel_id=1, source_target_pairs={{0,2},{2,0},{4,6},{6,4},{1,3},{3,1},{5,7},{7,5},{8,10},{10,8},{12,... | collective-permute-start | bytes 835592 | tf_op jit(solution)/shard_map/ppermute | solution.py:26
  225.1 37.7 %collective-permute-start.26 = (bf16[128,1088]{0,1:T(8,128)(2,1)}, bf16[128,1088]{0,1:T(8,128)(2,1)}, u32[]{:S(2)}, u32[]{:S(2)}) collective-permute-start(bf16[128,1088]{0,1:T(8,128)(2,1)} %get-tuple-element.66), channel_id=1, source_target_pairs={{0,6},{2,4},{4,2},{6,0},{1,7},{3,5},{5,3},{7,1},{8,14},{10,12},{12... | collective-permute-start | bytes 835592 | tf_op jit(solution)/shard_map/ppermute | solution.py:26
  239.5 32.0 %collective-permute-start.25 = (bf16[128,1088]{0,1:T(8,128)(2,1)}, bf16[128,1088]{0,1:T(8,128)(2,1)S(1)}, u32[]{:S(2)}, u32[]{:S(2)}) collective-permute-start(bf16[128,1088]{0,1:T(8,128)(2,1)} %get-tuple-element.67), channel_id=1, source_target_pairs={{0,4},{2,6},{4,0},{6,2},{1,5},{3,7},{5,1},{7,3},{8,12},{10,14},{12... | collective-permute-start | bytes 835592 | tf_op jit(solution)/shard_map/ppermute | solution.py:26
  274.1 44.8 %collective-permute-start.49 = (bf16[128,1088]{0,1:T(8,128)(2,1)}, bf16[128,1088]{0,1:T(8,128)(2,1)}, u32[]{:S(2)}, u32[]{:S(2)}) collective-permute-start(bf16[128,1088]{0,1:T(8,128)(2,1)} %get-tuple-element.50), channel_id=1, source_target_pairs={{0,6},{2,4},{4,2},{6,0},{1,7},{3,5},{5,3},{7,1},{8,14},{10,12},{12... | collective-permute-start | bytes 835592 | tf_op jit(solution)/shard_map/ppermute | solution.py:26
  275.4 44.0 %collective-permute-start.48 = (bf16[128,1088]{0,1:T(8,128)(2,1)}, bf16[128,1088]{0,1:T(8,128)(2,1)}, u32[]{:S(2)}, u32[]{:S(2)}) collective-permute-start(bf16[128,1088]{0,1:T(8,128)(2,1)} %get-tuple-element.50), channel_id=1, source_target_pairs={{0,4},{2,6},{4,0},{6,2},{1,5},{3,7},{5,1},{7,3},{8,12},{10,14},{12... | collective-permute-start | bytes 835592 | tf_op jit(solution)/shard_map/ppermute | solution.py:26
  275.4 44.1 %collective-permute-start.47 = (bf16[128,1088]{0,1:T(8,128)(2,1)}, bf16[128,1088]{0,1:T(8,128)(2,1)}, u32[]{:S(2)}, u32[]{:S(2)}) collective-permute-start(bf16[128,1088]{0,1:T(8,128)(2,1)} %get-tuple-element.50), channel_id=1, source_target_pairs={{0,2},{2,0},{4,6},{6,4},{1,3},{3,1},{5,7},{7,5},{8,10},{10,8},{12,... | collective-permute-start | bytes 835592 | tf_op jit(solution)/shard_map/ppermute | solution.py:26
  293.2 13.3 %collective-permute-start.36 = (bf16[128,320]{1,0:T(8,128)(2,1)S(1)}, bf16[128,320]{1,0:T(8,128)(2,1)S(1)}, u32[]{:S(2)}, u32[]{:S(2)}) collective-permute-start(bf16[128,320]{1,0:T(8,128)(2,1)S(1)} %get-tuple-element.81), channel_id=1, source_target_pairs={{0,4},{2,6},{4,0},{6,2},{1,5},{3,7},{5,1},{7,3},{8,12},{10,14},{12... | collective-permute-start | bytes 245768 | tf_op jit(solution)/shard_map/ppermute | solution.py:26
  298.8 9.5 %collective-permute-start.35 = (bf16[128,320]{1,0:T(8,128)(2,1)S(1)}, bf16[128,320]{1,0:T(8,128)(2,1)S(1)}, u32[]{:S(2)}, u32[]{:S(2)}) collective-permute-start(bf16[128,320]{1,0:T(8,128)(2,1)S(1)} %get-tuple-element.82), channel_id=1, source_target_pairs={{0,2},{2,0},{4,6},{6,4},{1,3},{3,1},{5,7},{7,5},{8,10},{10,8},{12,... | collective-permute-start | bytes 245768 | tf_op jit(solution)/shard_map/ppermute | solution.py:26
  306.5 48.0 %collective-permute-start.54 = (bf16[1088,544]{0,1:T(8,128)(2,1)}, bf16[1088,544]{0,1:T(8,128)(2,1)}, u32[]{:S(2)}, u32[]{:S(2)}) collective-permute-start(bf16[1088,544]{0,1:T(8,128)(2,1)} %split.60), channel_id=1, source_target_pairs={{0,1},{1,0},{2,3},{3,2},{4,5},{5,4},{6,7},{7,6},{8,9},{9,8},{10,11... | collective-permute-start | bytes 3551240 | tf_op jit(solution)/shard_map/ppermute | solution.py:26
  308.3 49.6 %collective-permute-start.53 = (bf16[544,1088]{1,0:T(8,128)(2,1)}, bf16[544,1088]{1,0:T(8,128)(2,1)}, u32[]{:S(2)}, u32[]{:S(2)}) collective-permute-start(bf16[544,1088]{1,0:T(8,128)(2,1)} %split.61), channel_id=1, source_target_pairs={{0,1},{1,0},{2,3},{3,2},{4,5},{5,4},{6,7},{7,6},{8,9},{9,8},{10,11... | collective-permute-start | bytes 3551240 | tf_op jit(solution)/shard_map/ppermute | solution.py:26
  319.4 18.5 %collective-permute-start.38 = (bf16[4,128,640]{2,1,0:T(8,128)(2,1)}, bf16[4,128,640]{2,1,0:T(8,128)(2,1)}, u32[]{:S(2)}, u32[]{:S(2)}) collective-permute-start(bf16[4,128,640]{2,1,0:T(8,128)(2,1)} %get-tuple-element.24), channel_id=1, source_target_pairs={{0,1},{1,0},{2,3},{3,2},{4,5},{5,4},{6,7},{7,6},{8,9},{9,8},{10,11... | collective-permute-start | bytes 1966088 | tf_op jit(solution)/shard_map/ppermute | solution.py:26
  348.6 12.6 %collective-permute-start.43 = (bf16[544,960]{1,0:T(8,128)(2,1)}, bf16[544,960]{1,0:T(8,128)(2,1)}, u32[]{:S(2)}, u32[]{:S(2)}) collective-permute-start(bf16[544,960]{1,0:T(8,128)(2,1)} %copy.64), channel_id=1, source_target_pairs={{0,1},{1,0},{2,3},{3,2},{4,5},{5,4},{6,7},{7,6},{8,9},{9,8},{10,11... | collective-permute-start | bytes 3133448 | tf_op jit(solution)/shard_map/ppermute | solution.py:26
  372.1 21.0 %collective-permute-start.45 = (bf16[544,304]{1,0:T(8,128)(2,1)S(1)}, bf16[544,304]{1,0:T(8,128)(2,1)S(1)}, u32[]{:S(2)}, u32[]{:S(2)}) collective-permute-start(bf16[544,304]{1,0:T(8,128)(2,1)S(1)} %fusion.24), channel_id=1, source_target_pairs={{0,4},{2,6},{4,0},{6,2},{1,5},{3,7},{5,1},{7,3},{8,12},{10,14},{12... | collective-permute-start | bytes 992264 | tf_op jit(solution)/shard_map/ppermute | solution.py:26
  373.9 23.7 %collective-permute-start.44 = (bf16[544,320]{1,0:T(8,128)(2,1)S(1)}, bf16[544,320]{1,0:T(8,128)(2,1)S(1)}, u32[]{:S(2)}, u32[]{:S(2)}) collective-permute-start(bf16[544,320]{1,0:T(8,128)(2,1)S(1)} %fusion.23), channel_id=1, source_target_pairs={{0,2},{2,0},{4,6},{6,4},{1,3},{3,1},{5,7},{7,5},{8,10},{10,8},{12,... | collective-permute-start | bytes 1044488 | tf_op jit(solution)/shard_map/ppermute | solution.py:26
  375.6 22.8 %collective-permute-start.46 = (bf16[544,48]{1,0:T(8,128)(2,1)S(1)}, bf16[544,48]{1,0:T(8,128)(2,1)S(1)}, u32[]{:S(2)}, u32[]{:S(2)}) collective-permute-start(bf16[544,48]{1,0:T(8,128)(2,1)S(1)} %convolution_convert_fusion.9), channel_id=1, source_target_pairs={{0,6},{2,4},{4,2},{6,0},{1,7},{3,5},{5,3},{7,1},{8,14},{10,12},{12... | collective-permute-start | bytes 156680 | tf_op jit(solution)/shard_map/ppermute | solution.py:26
  401.3 49.4 %collective-permute-start.39 = (bf16[128,1088]{0,1:T(8,128)(2,1)S(1)}, bf16[128,1088]{0,1:T(8,128)(2,1)S(1)}, u32[]{:S(2)}, u32[]{:S(2)}) collective-permute-start(bf16[128,1088]{0,1:T(8,128)(2,1)S(1)} %get-tuple-element.59), channel_id=1, source_target_pairs={{0,2},{2,0},{4,6},{6,4},{1,3},{3,1},{5,7},{7,5},{8,10},{10,8},{12,... | collective-permute-start | bytes 835592 | tf_op jit(solution)/shard_map/ppermute | solution.py:26
  402.4 48.4 %collective-permute-start.41 = (bf16[128,1088]{0,1:T(8,128)(2,1)S(1)}, bf16[128,1088]{0,1:T(8,128)(2,1)S(1)}, u32[]{:S(2)}, u32[]{:S(2)}) collective-permute-start(bf16[128,1088]{0,1:T(8,128)(2,1)S(1)} %get-tuple-element.60), channel_id=1, source_target_pairs={{0,6},{2,4},{4,2},{6,0},{1,7},{3,5},{5,3},{7,1},{8,14},{10,12},{12... | collective-permute-start | bytes 835592 | tf_op jit(solution)/shard_map/ppermute | solution.py:26
  405.0 45.7 %collective-permute-start.40 = (bf16[128,1088]{0,1:T(8,128)(2,1)S(1)}, bf16[128,1088]{0,1:T(8,128)(2,1)S(1)}, u32[]{:S(2)}, u32[]{:S(2)}) collective-permute-start(bf16[128,1088]{0,1:T(8,128)(2,1)S(1)} %get-tuple-element.61), channel_id=1, source_target_pairs={{0,4},{2,6},{4,0},{6,2},{1,5},{3,7},{5,1},{7,3},{8,12},{10,14},{12... | collective-permute-start | bytes 835592 | tf_op jit(solution)/shard_map/ppermute | solution.py:26
  (94 other events, 1460.1 us)
Sparse Core Ops, SparseCore 0:
  400.0 100.4 all-reduce.6
